TPU v7x, 256 devices: a whole 4x4x8 slice. The times are simulated.
256 devices in a mesh: tile: 32 (over x, z), band: 8 (over y, core).
Axes of the slice: x: 4, y: 4, z: 8, core: 2. Of those that a mesh axis runs over, the one named last changes fastest.
Arguments:
- members: bfloat16 [64, 128, 65536], P(None, 'band', 'tile'), may hold values from -6 to 6
- modes: float32 [8, 128], replicated, may hold values from -4 to 4
- obs_cell: int32 [2097152], P(('tile', 'band')), may hold values from 0 to 2047
- obs_level: int32 [2097152], P(('tile', 'band')), may hold values from 0 to 15
- obs_side: int32 [2097152], P(('tile', 'band')), may hold values from 0 to 1
- obs_weight: float32 [2097152], P(('tile', 'band')), may hold values from 0.1 to 0.9
- obs_scale: float32 [2097152], P(('tile', 'band')), may hold values from 0.01 to 0.05
- innovation: float32 [2097152], P(('tile', 'band')), may hold values from -6 to 6
Outputs:
- increment: float32 [128, 65536], P('band', 'tile')
- analysis: bfloat16 [64, 128, 65536], P(None, 'band', 'tile')
All inputs are finite; a program needn't handle non-finite values.
Results may differ from a plain program's by a relative error of at most 0.0087.
Values may be sent and summed in bfloat16 or wider, within the bound.
A program may use at most 128 MiB of HBM per device.

v0:
```python
import jax
import jax.numpy as jnp
from jax import lax
from jax.sharding import PartitionSpec as P


def padded_2(cells, sides, width):
    for axis, dim in sides:
        count = lax.axis_size(axis)
        ends = count - 1
        head = lax.slice_in_dim(cells, 0, width, axis=dim)
        tail = lax.slice_in_dim(cells, cells.shape[dim] - width, cells.shape[dim], axis=dim)
        cells = jnp.concatenate(
            [
                lax.ppermute(tail, axis, [(i, (i + 1) % count) for i in range(ends)]),
                cells,
                lax.ppermute(head, axis, [((i + 1) % count, i) for i in range(ends)]),
            ],
            axis=dim,
        )
    return cells


def per_device(members, modes, obs_cell, obs_level, obs_side, obs_weight, obs_scale, innovation):
    n_members = members.shape[0]
    lev_dev = members.shape[1]
    cells_dev = members.shape[2]
    n_modes = modes.shape[0]
    levels = modes.shape[1]
    ens = n_members * n_modes
    obs_dev = obs_cell.shape[0]
    band = lax.axis_index("band")
    padded = padded_2(members, (("band", 1),), 1)
    flat = padded.reshape(n_members, (lev_dev + 2) * cells_dev)
    offset = 2 * obs_side - 1
    near = jnp.take(flat, (obs_level + 1) * cells_dev + obs_cell, axis=1).astype(jnp.float32)
    far = jnp.take(flat, (obs_level + 1 + offset) * cells_dev + obs_cell, axis=1).astype(
        jnp.float32
    )
    near_level = band * lev_dev + obs_level
    far_level = near_level + offset
    grid = lax.iota(jnp.int32, levels)
    near_pick = (grid[:, None] == near_level[None, :]).astype(jnp.float32)
    far_pick = (grid[:, None] == far_level[None, :]).astype(jnp.float32)
    near_mode = jnp.dot(modes, near_pick, precision=lax.Precision.HIGHEST)
    far_mode = jnp.dot(modes, far_pick, precision=lax.Precision.HIGHEST)
    keep = 1.0 - obs_weight
    perturb = obs_scale * (
        keep * near[:, None, :] * near_mode[None] + obs_weight * far[:, None, :] * far_mode[None]
    )
    perturb = perturb.reshape(ens, obs_dev).astype(jnp.bfloat16)
    plain = (obs_scale * (keep * near + obs_weight * far)).astype(jnp.bfloat16)
    scaled = (obs_scale * innovation).astype(jnp.bfloat16)
    gram = lax.dot_general(
        perturb, perturb, (((1,), (1,)), ((), ())), preferred_element_type=jnp.float32
    )
    cross = lax.dot_general(
        perturb, plain, (((1,), (1,)), ((), ())), preferred_element_type=jnp.float32
    )
    drive = jnp.dot(perturb, scaled, preferred_element_type=jnp.float32)
    prior = float(ens - 1) * jnp.eye(ens, dtype=jnp.float32)
    gram, cross, drive = lax.psum((gram, cross, drive), ("tile", "band"))
    lower = jnp.linalg.cholesky(gram + prior)
    rhs = jnp.concatenate([drive[:, None], cross], axis=1)
    first = lax.linalg.triangular_solve(lower, rhs, left_side=True, lower=True)
    solved = lax.linalg.triangular_solve(lower, first, left_side=True, lower=True, transpose_a=True)
    local_modes = lax.dynamic_slice_in_dim(modes, band * lev_dev, lev_dev, 1)
    mean_weights = jnp.einsum(
        "pj,jl->lp",
        solved[:, 0].reshape(n_members, n_modes),
        local_modes,
        precision=lax.Precision.HIGHEST,
    ).astype(jnp.bfloat16)
    member_weights = jnp.einsum(
        "pjk,jl->lpk",
        solved[:, 1:].reshape(n_members, n_modes, n_members),
        local_modes,
        precision=lax.Precision.HIGHEST,
    ).astype(jnp.bfloat16)
    increment = jnp.einsum("lp,plc->lc", mean_weights, members, preferred_element_type=jnp.float32)
    correction = jnp.einsum(
        "lpk,plc->klc", member_weights, members, preferred_element_type=jnp.float32
    )
    analysis = (members.astype(jnp.float32) - correction).astype(jnp.bfloat16)
    return (increment, analysis)


def solution(mesh):
    placed = (
        P(None, "band", "tile"),
        P(),
        P(("tile", "band")),
        P(("tile", "band")),
        P(("tile", "band")),
        P(("tile", "band")),
        P(("tile", "band")),
        P(("tile", "band")),
    )
    return jax.shard_map(
        per_device,
        mesh=mesh,
        in_specs=placed,
        out_specs=(P("band", "tile"), P(None, "band", "tile")),
        check_vma=False,
    )
```

profile of v0, /device:TPU:1, one launch (start us, length us, event | category | flops | bytes accessed | tf_op | source)
XLA Modules:
  0.0 551.1 jit_solution(4017757446916398105)
XLA Ops:
  7.2 3.2 fusion.95
  10.6 4.6 collective-permute-start
  19.7 2.1 convolution_bitcast_fusion
  24.8 7.4 %pad_maximum_fusion = bf16[64,18,2048]{2,1,0:T(8,128)(2,1)} fusion(bf16[64,1,2048]{2,1,0:T(2,128)(2,1)S(1)} %copy.68, bf16[64,16,2048]{2,1,0:T(8,128)(2,1)} %param.10, bf16[64,1,2048]{2,1,0:T(2,128)(2,1)S(1)} %copy.67), kind=kLoop, calls=%fused_computation.31 | loop fusion | flops 14155776 | bytes 9437184 | tf_op jit(solution)/shard_map/concatenate | solution.py:13
  32.2 12.6 %copy.69 = bf16[64,18,2048]{0,2,1:T(8,128)(2,1)} copy(bf16[64,18,2048]{2,1,0:T(8,128)(2,1)} %pad_maximum_fusion) | data formatting | bytes 9437184 | tf_op jit(solution)/shard_map/concatenate | solution.py:13
  44.8 26.8 %gather_fusion = bf16[8192,64]{1,0:T(8,128)(2,1)S(1)} fusion(bf16[64,36864]{0,1:T(8,128)(2,1)} %bitcast.97, s32[8192]{0:T(1024)S(1)} %get-tuple-element.59), kind=kCustom, calls=%fused_computation.clone | custom fusion | bytes 2129920 | tf_op jit(solution)/shard_map/jit(_take)/gather | solution.py:36
  72.5 26.9 %gather_fusion.1 = bf16[8192,64]{1,0:T(8,128)(2,1)S(1)} fusion(bf16[64,36864]{0,1:T(8,128)(2,1)} %bitcast.98, s32[8192]{0:T(1024)S(1)} %get-tuple-element.60), kind=kCustom, calls=%fused_computation.1.clone | custom fusion | bytes 2129920 | tf_op jit(solution)/shard_map/jit(_take)/gather | solution.py:37
  103.0 3.7 fusion.1
  106.7 9.5 %fusion.6 = f32[512,512]{0,1:T(8,128)} fusion(f32[8,8192]{1,0:T(8,128)S(1)} %copy-done.7, f32[64,8192]{1,0:T(8,128)S(1)} %get-tuple-element.63, f32[8,8192]{1,0:T(8,128)S(1)} %copy-done.9, f32[64,8192]{1,0:T(8,128)S(1)} %get-tuple-element.64, f32[8192]{0:T(1024)S(1)} %copy-done.6), kind=kOutput, calls=%fused_computation.13 | convolution fusion | flops 4315938816 | bytes 5799936 | tf_op jit(solution)/shard_map/dot_general | solution.py:54
  116.3 4.7 fusion.27
  121.0 80.9 %psum.22 = f32[512,1]{0,1:T(1,128)S(1)} all-reduce(f32[512,1]{0,1:T(1,128)S(1)} %fusion.27), channel_id=1, replica_groups=mesh['tile'=32,'band'=8] {'tile','band'}, use_global_device_ids=true, to_apply=%region_9.11 | all-reduce | flops 512 | bytes 4096 | tf_op jit(solution)/shard_map/psum | solution.py:62
  201.9 173.8 %all-reduce.4.cloned.1.call-done = (f32[512,512]{0,1:T(8,128)}, f32[512,64]{0,1:T(8,128)}) async-done(((f32[512,512]{0,1:T(8,128)}, f32[512,64]{0,1:T(8,128)}), (f32[512,512]{0,1:T(8,128)}, f32[512,64]{0,1:T(8,128)})) %all-reduce.4.cloned.1.call-update) | async-done | bytes 1179664 | tf_op jit(solution)/shard_map/psum | solution.py:62
  377.7 11.7 %cholesky.103 = f32[128,128]{1,0:T(8,128)S(1)} custom-call(f32[128,128]{1,0:T(8,128)S(1)} %cholesky.263), custom_call_target="Cholesky" | custom-call | tf_op jit(solution)/shard_map/jit(cholesky)/cholesky | solution.py:63
  389.4 9.8 %custom-call.32 = f32[1,128,128]{1,2,0:T(8,128)S(1)} custom-call(f32[1,128,128]{2,1,0:T(8,128)S(1)} %get-tuple-element.56), custom_call_target="InvertDiagBlocksLowerTriangular" | custom-call | tf_op jit(solution)/shard_map/jit(cholesky)/cholesky | solution.py:63
  399.9 11.7 %cholesky.215 = f32[128,128]{1,0:T(8,128)S(1)} custom-call(f32[128,128]{1,0:T(8,128)S(1)} %cholesky.267), custom_call_target="Cholesky" | custom-call | tf_op jit(solution)/shard_map/jit(cholesky)/cholesky | solution.py:63
  412.0 9.9 %custom-call.33 = f32[1,128,128]{1,2,0:T(8,128)S(1)} custom-call(f32[1,128,128]{2,1,0:T(8,128)S(1)} %get-tuple-element.54), custom_call_target="InvertDiagBlocksLowerTriangular" | custom-call | tf_op jit(solution)/shard_map/jit(cholesky)/cholesky | solution.py:63
  423.1 11.7 %cholesky.236 = f32[128,128]{1,0:T(8,128)S(1)} custom-call(f32[128,128]{1,0:T(8,128)S(1)} %cholesky.272), custom_call_target="Cholesky" | custom-call | tf_op jit(solution)/shard_map/jit(cholesky)/cholesky | solution.py:63
  434.9 9.8 %custom-call.34 = f32[1,128,128]{1,2,0:T(8,128)S(1)} custom-call(f32[1,128,128]{2,1,0:T(8,128)S(1)} %get-tuple-element.52), custom_call_target="InvertDiagBlocksLowerTriangular" | custom-call | tf_op jit(solution)/shard_map/jit(cholesky)/cholesky | solution.py:63
  445.5 11.9 %cholesky.253 = f32[128,128]{1,0:T(8,128)S(1)} custom-call(f32[128,128]{1,0:T(8,128)S(1)} %convolution_subtract_fusion.2), custom_call_target="Cholesky" | custom-call | tf_op jit(solution)/shard_map/jit(cholesky)/cholesky | solution.py:63
  462.8 10.8 %while.1 = (s32[]{:T(128)}, f32[512,512]{0,1:T(8,128)S(1)}, s32[4,2]{0,1:T(2,128)S(1)}, f32[4,128,128]{2,1,0:T(8,128)}, s32[]{:T(128)}) while((s32[]{:T(128)}, f32[512,512]{0,1:T(8,128)S(1)}, s32[4,2]{0,1:T(2,128)S(1)}, f32[4,128,128]{2,1,0:T(8,128)}, s32[]{:T(128)}) %tuple.42), condition=%wide.while_cond, body=%wide.while_body.sunk | while | flops 2 | bytes 393829 | solution.py:66
  473.6 40.1 %custom-call.35 = f32[4,128,128]{1,2,0:T(8,128)S(1)} custom-call(f32[4,128,128]{2,1,0:T(8,128)} %get-tuple-element.10), custom_call_target="InvertDiagBlocksLowerTriangular" | custom-call | tf_op jit(solution)/shard_map/triangular_solve | solution.py:66
  518.3 13.5 %fusion.8 = bf16[64,16,2048]{2,0,1:T(8,128)(2,1)S(1)} fusion(bf16[16,64,64]{2,0,1:T(8,128)(2,1)S(1)} %convolution_convert_fusion, bf16[64,16,2048]{2,1,0:T(8,128)(2,1)} %param.10), kind=kOutput, calls=%fused_computation.15 | convolution fusion | flops 274726912 | bytes 8519680 | tf_op jit(solution)/shard_map/lpk,plc->klc/dot_general | solution.py:81
  531.8 4.3 copy.86
  536.4 6.7 %fusion.80 = f32[16,1,2048]{2,1,0:T(1,128)S(1)} fusion(bf16[16,64,1]{1,0,2:T(8,128)(2,1)S(1)} %fusion.26, bf16[64,16,2048]{2,1,0:T(8,128)(2,1)} %param.10), kind=kOutput, calls=%fused_computation.142 | convolution fusion | flops 4194304 | bytes 4327424 | tf_op jit(solution)/shard_map/lp,plc->lc/dot_general | solution.py:80
  (115 shorter events, 36.1 us)
Async XLA Ops:
  7.2 12.5 %copy-start = (f32[8,128]{1,0:T(8,128)S(1)}, f32[8,128]{1,0:T(8,128)}, u32[]{:S(2)}) copy-start(f32[8,128]{1,0:T(8,128)} %param.11) | copy-start | bytes 12292
  7.2 14.6 %copy-start.6 = (f32[8192]{0:T(1024)S(1)}, f32[8192]{0:T(1024)}, u32[]{:S(2)}) copy-start(f32[8192]{0:T(1024)} %param.16) | copy-start | bytes 98308
  7.2 14.6 %copy-start.5 = (f32[8192]{0:T(1024)S(1)}, f32[8192]{0:T(1024)}, u32[]{:S(2)}) copy-start(f32[8192]{0:T(1024)} %param.17) | copy-start | bytes 98308
  7.2 368.5 %all-reduce.4.cloned.1.call-start = ((), (), s32[]{:S(2)}) async-start(), calls=%async_computation | async-start | bytes 2359296 | tf_op jit(solution)/shard_map/psum | solution.py:62
  10.6 13.4 %collective-permute-start = (bf16[64,1,2048]{2,0,1:T(8,128)(2,1)S(1)}, bf16[64,1,2048]{2,0,1:T(8,128)(2,1)S(1)}, u32[]{:S(2)}, u32[]{:S(2)}) collective-permute-start(bf16[64,1,2048]{2,0,1:T(8,128)(2,1)S(1)} %copy.103), channel_id=1, source_target_pairs={{0,1},{1,2},{2,3},{3,4},{4,5},{5,6},{6,7},{8,9},{9,10},{10,11},{11... | collective-permute-start | bytes 786440 | tf_op jit(solution)/shard_map/ppermute | solution.py:15
  15.3 9.0 %collective-permute-start.1 = (bf16[64,1,2048]{2,0,1:T(8,128)(2,1)S(1)}, bf16[64,1,2048]{2,0,1:T(8,128)(2,1)S(1)}, u32[]{:S(2)}, u32[]{:S(2)}) collective-permute-start(bf16[64,1,2048]{2,0,1:T(8,128)(2,1)S(1)} %copy.102), channel_id=1, source_target_pairs={{1,0},{2,1},{3,2},{4,3},{5,4},{6,5},{7,6},{9,8},{10,9},{11,10},{12... | collective-permute-start | bytes 786440 | tf_op jit(solution)/shard_map/ppermute | solution.py:17
  72.5 28.5 %copy-start.4 = (f32[8192]{0:T(1024)S(1)}, f32[8192]{0:T(1024)}, u32[]{:S(2)}) copy-start(f32[8192]{0:T(1024)} %param.15) | copy-start | bytes 98308
  101.0 1.9 copy-start.7
  101.0 1.9 copy-start.9
  103.0 3.8 copy-start.2
  106.7 9.6 %copy-start.8 = (f32[8,8192]{1,0:T(8,128)S(1)}, f32[8,8192]{1,0:T(8,128)}, u32[]{:S(2)}) copy-start(f32[8,8192]{1,0:T(8,128)} %convolution_bitcast_fusion) | copy-start | bytes 786436
  106.7 9.6 %copy-start.10 = (f32[8,8192]{1,0:T(8,128)S(1)}, f32[8,8192]{1,0:T(8,128)}, u32[]{:S(2)}) copy-start(f32[8,8192]{1,0:T(8,128)} %convolution_bitcast_fusion.1) | copy-start | bytes 786436
  375.7 1.8 copy-start.1
  411.9 101.8 %copy-start.3 = (f32[512,64]{0,1:T(8,128)S(1)}, f32[512,64]{0,1:T(8,128)}, u32[]{:S(2)}) copy-start(f32[512,64]{0,1:T(8,128)} %get-tuple-element.44) | copy-start | bytes 393220
Sparse Core Ops, SparseCore 0:
  116.4 259.2 all-reduce.3
where the time goes:
time: 558 us; the launch traced here: 551 us
  waiting for transfers between devices  174 us (31%)
  other arithmetic  133 us (24%)
  local copies, waits for them, and re-layouts  90.1 us (16%)
  blocking collectives  80.9 us (14%)
  matrix products  49.3 us (9%)
  between operations  17.5 us (3%)
  starting transfers between devices  6.55 us (1%)
    psum x1, waiting for transfers between devices, per_device(): gram, cross, drive = lax.psum((gram, cross, drive), ('tile', 'band'))  174 us
    psum x1, blocking collectives, per_device(): gram, cross, drive = lax.psum((gram, cross, drive), ('tile', 'band'))  80.9 us
    another operation x15, other arithmetic, per_device(): lower = jnp.linalg.cholesky(gram + prior)  79.3 us
    another operation x4, other arithmetic, per_device(): lax.linalg.triangular_solve(lower, first, left_side=True, lower=True, tra...  40.3 us
    gather x2, local copies, waits for them, and re-layouts, per_device(): jnp.take(flat, (obs_level + 1 + offset) * cells_dev + obs_cell, axis=1)  28.5 us
    gather x2, local copies, waits for them, and re-layouts, per_device(): jnp.take(flat, (obs_level + 1) * cells_dev + obs_cell, axis=1)  27.7 us
    dot_general x1, matrix products, per_device(): jnp.einsum('lpk,plc->klc', member_weights, members, preferred_element_typ...  13.5 us
    concatenate x1, local copies, waits for them, and re-layouts, padded_2(): jnp.concatenate([lax.ppermute(tail, axis, [(i, (i + 1) % count) for i in...  12.6 us
  transfers between devices with their start and end apart: 3, of which 1 were waited for; matrix products, arithmetic and copies ran while one was open for 2% of the time, Pallas kernels for 0%

commit v1 on v0

v1 whole, which is shorter than its diff:
```python
import jax
import jax.numpy as jnp
from jax import lax
from jax.experimental import pallas as pl
from jax.experimental.pallas import tpu as pltpu
from jax.sharding import PartitionSpec as P

BF = jnp.bfloat16
F32 = jnp.float32
VM = pl.BlockSpec(memory_space=pltpu.VMEM)
NT = (((1,), (1,)), ((), ()))
ROWS = 1792
HALF = ROWS // 2
PIECE = HALF // 16


def scatter_kernel(cell_ref, level_ref, side_ref, weight_ref, scale_ref, innov_ref, field_ref, lhs_s, hot_s):
    field_ref[...] = jnp.zeros_like(field_ref)
    rows16 = lax.broadcasted_iota(jnp.int32, (16, 128), 0).astype(F32)
    zero = jnp.zeros((16, 128), BF)
    one = jnp.ones((16, 128), BF)

    def chunk(i, _):
        sl = pl.ds(pl.multiple_of(i * 8, 8), 8)
        cell = cell_ref[sl, :]
        lev = level_ref[sl, :]
        side = side_ref[sl, :]
        w = weight_ref[sl, :]
        s = scale_ref[sl, :]
        ch = cell >> 8
        cl8 = (cell & 255).astype(F32)
        kn8 = ((lev + 1) * 8 + ch).astype(F32)
        kf8 = ((lev + 2 * side) * 8 + ch).astype(F32)
        kp8 = ((lev + side) * 8 + ch).astype(F32)
        a = s * (1.0 - w)
        b = s * w
        t = s * innov_ref[sl, :]

        def split(v):
            hi = v.astype(BF).astype(F32)
            return hi, v - hi

        vals = [split(v) for v in (a * a, b * b, a * b, a * t, b * t)]
        for k in range(8):
            cols = slice(128 * k, 128 * k + 128)

            def wide(v):
                return jnp.broadcast_to(v[k : k + 1, :], (16, 128)).astype(BF)

            cl, kn, kf, kp = wide(cl8), wide(kn8), wide(kf8), wide(kp8)
            dn, df, e, gn, gf = [(wide(h), wide(l)) for h, l in vals]
            for g in range(9):
                it = (rows16 + 16.0 * g).astype(BF)
                mn = it == kn
                mf = it == kf
                mp = it == kp
                for h in range(2):
                    at = 144 * h + 16 * g
                    lhs_s[pl.ds(at, 16), cols] = jnp.where(mn, dn[h], jnp.where(mf, df[h], zero))
                    lhs_s[pl.ds(288 + at, 16), cols] = jnp.where(mn, gn[h], jnp.where(mf, gf[h], zero))
                    lhs_s[pl.ds(576 + at, 16), cols] = jnp.where(mp, e[h], zero)
            for g in range(16):
                it = (rows16 + 16.0 * g).astype(BF)
                hot_s[pl.ds(16 * g, 16), cols] = jnp.where(it == cl, one, zero)
        field_ref[...] += lax.dot_general(lhs_s[...], hot_s[...], NT, preferred_element_type=F32)
        return 0

    lax.fori_loop(0, 8, chunk, 0)


def sums_kernel(field_ref, mem_ref, lo_ref, hi_ref, modes_ref, out_ref, x32_s, stack_s, prod_s, coef_s):
    def conv(m, _):
        v = mem_ref[m].astype(F32)
        for k in range(16):
            x32_s[k, pl.ds(pl.multiple_of(m * 16, 16), 16), :] = v[:, 128 * k:128 * k + 128]
        return 0
    lax.fori_loop(0, 64, conv, 0, unroll=2)

    first = lax.broadcasted_iota(jnp.int32, (16, 128), 0)

    def level(r, k):
        if r == 0:
            return lo_ref[:, 128 * k:128 * k + 128].astype(F32)
        if r == 17:
            return hi_ref[:, 128 * k:128 * k + 128].astype(F32)
        return x32_s[k, pl.ds(r - 1, 64, stride=16), :]

    def field(f, r, k):
        row, ls = 288 * f + 8 * r + k // 2, slice(128 * (k % 2), 128 * (k % 2) + 128)
        return field_ref[pl.ds(row, 1), ls] + field_ref[pl.ds(row + 144, 1), ls]

    for q in range(9):
        for k in range(16):
            cs = slice(128 * k, 128 * k + 128)
            xs = {r: level(r, k) for r in range(max(2 * q - 1, 0), min(2 * q + 3, 18))}
            es = {r: field(2, r, k) for r in range(max(2 * q - 1, 0), min(2 * q + 2, 17))}
            for h in range(2):
                r = 2 * q + h
                base = 208 * h
                x = xs[r]
                stack_s[pl.ds(416 + 64 * h, 64), cs] = x.astype(BF)
                stack_s[pl.ds(base, 64), cs] = (x * field(0, r, k)).astype(BF)
                zero = jnp.zeros((64, 128), BF)
                stack_s[pl.ds(base + 64, 64), cs] = (xs[r - 1] * es[r - 1]).astype(BF) if r > 0 else zero
                stack_s[pl.ds(base + 128, 64), cs] = (xs[r + 1] * es[r]).astype(BF) if r < 17 else zero
                g = jnp.broadcast_to(field(1, r, k), (16, 128))
                gh = g.astype(BF).astype(F32)
                stack_s[pl.ds(base + 192, 16), cs] = jnp.where(first == 0, gh, jnp.where(first == 1, g - gh, 0.0)).astype(BF)
        p = lax.dot_general(stack_s[pl.ds(0, 416), :], stack_s[pl.ds(416, 128), :], (((1,), (1,)), ((), ())),
                            preferred_element_type=F32)
        lane = lax.broadcasted_iota(jnp.int32, (208, 128), 1)
        prod_s[q] = jnp.where(lane < 64, p[:208], p[208:])

    start = lax.axis_index("band") * 16 - 1
    half = lax.broadcasted_iota(jnp.int32, (1, 128), 1) < 64
    for j in range(9):
        if j < 8:
            phi = []
            for r in range(-1, 19):
                l = start + r
                ok = (l >= 0) & (l < 128)
                phi.append(jnp.where(ok, modes_ref[j, jnp.clip(l, 0, 127)], 0.0))
        else:
            phi = [jnp.float32(1.0)] * 20
        for q in range(9):
            for s in range(3):
                r = 2 * q + (1, 0, 2)[s]
                coef_s[s, j, pl.ds(q, 1), :] = jnp.where(half, phi[r], phi[r + 1])
    lane8 = lax.broadcasted_iota(jnp.int32, (8, 128), 1) < 64
    def group(i, _):
        s0 = [prod_s[q, pl.ds(i * 8, 8), :] for q in range(9)]
        s1 = [prod_s[q, pl.ds(64 + i * 8, 8), :] for q in range(9)]
        s2 = [prod_s[q, pl.ds(128 + i * 8, 8), :] for q in range(9)]
        row = 0
        for j in range(8):
            t = [s0[q] * coef_s[0, j, pl.ds(q, 1), :] + s1[q] * coef_s[1, j, pl.ds(q, 1), :] + s2[q] * coef_s[2, j, pl.ds(q, 1), :] for q in range(9)]
            def block(jj):
                acc = t[0] * coef_s[0, jj, pl.ds(0, 1), :]
                for q in range(1, 9):
                    acc = acc + t[q] * coef_s[0, jj, pl.ds(q, 1), :]
                return acc
            for pair in range(j // 2, 5):
                u = block(2 * pair)
                u = u + pltpu.roll(u, 64, 1)
                if pair < 4:
                    v = block(2 * pair + 1)
                    v = v + pltpu.roll(v, 64, 1)
                    u = jnp.where(lane8, u, v)
                else:
                    u = jnp.where(lane8, u, 0.0)
                out_ref[pl.ds(row * 64 + i * 8, 8), :] = u
                row += 1
        return 0
    lax.fori_loop(0, 8, group, 0)
    row = 0
    for j in range(8):
        row += 5 - j // 2
        dr = jnp.zeros((1, 128), F32)
        for q in range(9):
            g = prod_s[q, pl.ds(192, 8), :]
            dr = dr + (g[0:1] + g[1:2]) * coef_s[0, j, pl.ds(q, 1), :]
        dr = dr + pltpu.roll(dr, 64, 1)
        at = (row - 1) * 64
        old = out_ref[pl.ds(at, 8), :]
        keep = lane8 | (lax.broadcasted_iota(jnp.int32, (8, 128), 0) > 0)
        out_ref[pl.ds(at, 8), :] = jnp.where(keep, old, jnp.broadcast_to(dr, (8, 128)))


def reduce_kernel(in_ref, out_ref, from_core, acc_s, from_plane, from_line, send1, recv1, send2, recv2, send3, recv3, send4, recv4, send5, recv5):
    tile = lax.axis_index("tile")
    band = lax.axis_index("band")
    x, z, y, core = tile // 8, tile % 8, band // 2, band % 2

    def dev(xx, yy, zz, cc):
        return (xx * 8 + zz, yy * 2 + cc)

    def plane(e):
        return (x + e // 4) % 4, (y + e % 4) % 4

    order = sorted(range(1, 16), key=lambda e: -(min(e // 4, 4 - e // 4) + min(e % 4, 4 - e % 4)))
    sibling = dev(x, y, z, 1 - core)
    partners = [sibling]
    for e in range(1, 16):
        xx, yy = plane(e)
        partners.append(dev(xx, yy, z, core))
    for e in range(1, 8):
        partners.append(dev(x, y, (z + e) % 8, core))
    barrier = pltpu.get_barrier_semaphore()
    for d in partners:
        pl.semaphore_signal(barrier, inc=1, device_id=d, device_id_type=pl.DeviceIdType.MESH)
    pl.semaphore_wait(barrier, len(partners))

    def copy(src, dst, ss, rs, d):
        return pltpu.make_async_remote_copy(src_ref=src, dst_ref=dst, send_sem=ss, recv_sem=rs, device_id=d,
                                            device_id_type=pl.DeviceIdType.MESH)

    mine = core * HALF
    other = (1 - core) * HALF
    part = HALF // 4
    step1 = []
    for i in range(4):
        c = copy(in_ref.at[pl.ds(pl.multiple_of(other + i * part, 8), part)], from_core.at[pl.ds(i * part, part)],
                 send1.at[i], recv1.at[i], sibling)
        c.start()
        step1.append(c)
    for i in range(4):
        step1[i].wait_recv()
        acc_s[pl.ds(i * part, part), :] = in_ref[pl.ds(pl.multiple_of(mine + i * part, 8), part), :] + from_core[pl.ds(i * part, part), :]

    place = x * 4 + y
    step2 = []
    for e in order:
        xx, yy = plane(e)
        c = copy(acc_s.at[pl.ds(pl.multiple_of((xx * 4 + yy) * PIECE, 8), PIECE)], from_plane.at[e],
                 send2.at[e], recv2.at[e], dev(xx, yy, z, core))
        c.start()
        step2.append(c)
    total = acc_s[pl.ds(pl.multiple_of(place * PIECE, 8), PIECE), :]
    for e, c in zip(order, step2):
        c.wait_recv()
        total = total + from_plane[e]
    from_line[z] = total

    step3 = []
    for e in (4, 3, 5, 2, 6, 1, 7):
        c = copy(from_line.at[z], from_line.at[z], send3.at[e], recv3.at[e], dev(x, y, (z + e) % 8, core))
        c.start()
        step3.append(c)
    for c in step3:
        c.wait_recv()
    total = from_line[0]
    for e in range(1, 8):
        total = total + from_line[e]
    at = pl.multiple_of(mine + place * PIECE, 8)
    out_ref[pl.ds(at, PIECE), :] = total

    step4 = []
    for e in order:
        xx, yy = plane(e)
        c = copy(out_ref.at[pl.ds(at, PIECE)], out_ref.at[pl.ds(at, PIECE)], send4.at[e], recv4.at[e], dev(xx, yy, z, core))
        c.start()
        step4.append(c)
    step5 = []
    c = copy(out_ref.at[pl.ds(at, PIECE)], out_ref.at[pl.ds(at, PIECE)], send5.at[0], recv5.at[0], sibling)
    c.start()
    step5.append(c)
    for e, c4 in reversed(list(zip(order, step4))):
        c4.wait_recv()
        xx, yy = (x + 4 - e // 4) % 4, (y + 4 - e % 4) % 4
        here = pl.multiple_of(mine + (xx * 4 + yy) * PIECE, 8)
        c = copy(out_ref.at[pl.ds(here, PIECE)], out_ref.at[pl.ds(here, PIECE)], send5.at[e], recv5.at[e], sibling)
        c.start()
        step5.append(c)
    for c in step5:
        c.wait_recv()
    for c in step1 + step2 + step3 + step4 + step5:
        c.wait_send()


def dot(a, b, dims=(((1,), (0,)), ((), ()))):
    return lax.dot_general(a, b, dims, precision=lax.Precision.HIGHEST, preferred_element_type=F32)

def invert(m):
    lane = lax.broadcasted_iota(jnp.int32, (8, 128), 1)
    sub = lax.broadcasted_iota(jnp.int32, (8, 128), 0)
    def col(v, c):
        return jnp.broadcast_to(v[:, c:c + 1], (8, 128))
    def rowb(v, c):
        return jnp.broadcast_to(v[c:c + 1, :], (8, 128))
    for p in range(16):
        b = m[p]
        v = [col(b, 8 * p + c) for c in range(8)]
        for c in range(8):
            d = 1.0 / rowb(v[c], c)
            here = sub == c
            for e in range(c + 1, 8):
                r = rowb(v[e], c)
                v[e] = jnp.where(here, v[e] * d, v[e] - (v[c] * r) * d)
            at = lane == 8 * p + c
            r = jnp.where(at, 1.0, rowb(b, c)) * d
            b = jnp.where(here, r, jnp.where(at, 0.0, b) - v[c] * r)
        rows = [rowb(b, c) for c in range(8)]
        panel = (lane >= 8 * p) & (lane < 8 * p + 8)
        order = [i % 16 for i in range(p + 1, p + 16)]
        new = list(m)
        new[p] = b
        for i in order:
            terms = [col(m[i], 8 * p + c) * rows[c] for c in range(8)]
            while len(terms) > 1:
                terms = [x + y for x, y in zip(terms[::2], terms[1::2])]
            new[i] = jnp.where(panel, 0.0, m[i]) - terms[0]
        m = new
    return m

def solve(red_ref, a_s, w_s):
    lane = lax.broadcasted_iota(jnp.int32, (64, 128), 1)
    sub = lax.broadcasted_iota(jnp.int32, (64, 128), 0)
    row = 0
    for j in range(8):
        for pair in range(j // 2, 5):
            u = red_ref[pl.ds(64 * row, 64), :]
            if pair == j // 2:
                u = jnp.where(lane == sub + 64 * (j % 2), u + 511.0, u)
            if pair == 4:
                r = jnp.broadcast_to(u[0:1, :], (64, 128))
                drive = jnp.sum(jnp.where(lane == sub + 64, r, 0.0), axis=1, keepdims=True)
                u = jnp.where(lane < 64, u, jnp.where(lane == 64, drive, 0.0))
            a_s[pl.ds(64 * j, 64), pl.ds(128 * pair, 128)] = u
            row += 1
    for k in range(4):
        at = 128 * k
        m = [a_s[pl.ds(at + 8 * i, 8), pl.ds(at, 128)] for i in range(16)]
        inv = jnp.concatenate(invert(m), axis=0)
        w = dot(inv, a_s[pl.ds(at, 128), pl.ds(at + 128, 512 - at)])
        w_s[pl.ds(at, 128), pl.ds(at + 128, 512 - at)] = w
        for i in range(k + 1, 4):
            ki = a_s[pl.ds(at, 128), pl.ds(128 * i, 128)]
            a_s[pl.ds(128 * i, 128), pl.ds(128 * i, 640 - 128 * i)] -= dot(
                ki, w[:, 128 * (i - k - 1):], (((0,), (0,)), ((), ())))
    for k in (2, 1, 0):
        at = 128 * k
        w_s[pl.ds(at, 128), pl.ds(512, 128)] -= dot(
            w_s[pl.ds(at, 128), pl.ds(at + 128, 384 - at)], w_s[pl.ds(at + 128, 384 - at), pl.ds(512, 128)])


def update_kernel(red_ref, modes_ref, mem_hbm, inc_ref, ana_hbm, a_s, w_s, phi_s, u_s, big_s, mem_s, ana_s, load_sem, save_sem):
    load = pltpu.make_async_copy(mem_hbm, mem_s, load_sem)
    load.start()
    solve(red_ref, a_s, w_s)
    shift = lax.rem(128 - lax.axis_index("band") * 16, 128)
    phi = pltpu.roll(modes_ref[...], shift, 1)
    lane = lax.broadcasted_iota(jnp.int32, (8, 128), 1)
    for width in (16, 32, 64):
        phi = jnp.where(lane < width, phi, jnp.where(lane < 2 * width, pltpu.roll(phi, width, 1), 0.0))
    member = lax.broadcasted_iota(jnp.int32, (64, 1024), 0)
    owner = lax.broadcasted_iota(jnp.int32, (64, 1024), 1) // 16
    for j in range(8):
        wide = jnp.concatenate([jnp.broadcast_to(phi[j : j + 1, :], (64, 128))] * 8, axis=1)
        phi_s[pl.ds(64 * j, 64), :] = jnp.where(member == owner, wide, 0.0)
    u_s[...] = dot(w_s[:, 512:640], phi_s[...], (((0,), (0,)), ((), ())))
    level = lax.broadcasted_iota(jnp.int32, (16, 1024), 1) % 16
    own = level == lax.broadcasted_iota(jnp.int32, (16, 1024), 0)

    def spread(k, _):
        row = jnp.broadcast_to(u_s[pl.ds(k, 1), :], (16, 1024))
        big_s[pl.ds(pl.multiple_of(k * 16, 16), 16), :] = jnp.where(own, row, 0.0).astype(BF)
        return 0

    lax.fori_loop(0, 65, spread, 0, unroll=5)
    load.wait()
    saves = []
    for i in range(4):
        cols = pl.ds(512 * i, 512)
        m = mem_s[:, cols]
        r = jnp.dot(big_s[...], m, preferred_element_type=F32)
        ana_s[:, cols] = (m.astype(F32) - r[:1024]).astype(BF)
        inc_ref[:, cols] = r[1024:]
        save = pltpu.make_async_copy(ana_s.at[:, cols], ana_hbm.at[:, cols], save_sem.at[i])
        save.start()
        saves.append(save)
    for save in saves:
        save.wait()


def per_device(members, modes, *obs):
    def beside(a, forward):
        count = lax.axis_size("band")
        pairs = [(i, i + 1) if forward else (i + 1, i) for i in range(count - 1)]
        return lax.ppermute(a, "band", pairs)

    lo = beside(members[:, 15, :], True)
    hi = beside(members[:, 0, :], False)
    obs = [o.reshape(64, 128) for o in obs]
    field = pl.pallas_call(
        scatter_kernel,
        out_shape=jax.ShapeDtypeStruct((864, 256), F32),
        in_specs=[VM] * 6,
        out_specs=VM,
        scratch_shapes=[pltpu.VMEM((864, 1024), BF), pltpu.VMEM((256, 1024), BF)],
        compiler_params=pltpu.CompilerParams(vmem_limit_bytes=32 * 2**20),
        cost_estimate=pl.CostEstimate(flops=8 * 10**9, bytes_accessed=2**20, transcendentals=0),
        name="scatter",
    )(*obs)
    part = pl.pallas_call(
        sums_kernel,
        out_shape=jax.ShapeDtypeStruct((ROWS, 128), F32),
        in_specs=[VM] * 4 + [pl.BlockSpec(memory_space=pltpu.SMEM)],
        out_specs=VM,
        scratch_shapes=[
            pltpu.VMEM((16, 1024, 128), F32),
            pltpu.VMEM((544, 2048), BF),
            pltpu.VMEM((9, 208, 128), F32),
            pltpu.VMEM((3, 9, 9, 128), F32),
        ],
        compiler_params=pltpu.CompilerParams(vmem_limit_bytes=48 * 2**20),
        name="sums",
    )(field, members, lo, hi, modes)
    red = pl.pallas_call(
        reduce_kernel,
        out_shape=jax.ShapeDtypeStruct((ROWS, 128), F32),
        in_specs=[VM],
        out_specs=VM,
        scratch_shapes=[
            pltpu.VMEM((HALF, 128), F32),
            pltpu.VMEM((HALF, 128), F32),
            pltpu.VMEM((16, PIECE, 128), F32),
            pltpu.VMEM((8, PIECE, 128), F32),
        ]
        + [pltpu.SemaphoreType.DMA((n,)) for n in (4, 4, 16, 16, 8, 8, 16, 16, 16, 16)],
        compiler_params=pltpu.CompilerParams(
            collective_id=0, has_side_effects=True, vmem_limit_bytes=32 * 2**20
        ),
        name="reduce",
    )(part)
    inc, ana = pl.pallas_call(
        update_kernel,
        out_shape=(jax.ShapeDtypeStruct((16, 2048), F32), jax.ShapeDtypeStruct((1024, 2048), BF)),
        in_specs=[VM, VM, pl.BlockSpec(memory_space=pl.ANY)],
        out_specs=(VM, pl.BlockSpec(memory_space=pl.ANY)),
        scratch_shapes=[
            pltpu.VMEM((512, 640), F32),
            pltpu.VMEM((512, 640), F32),
            pltpu.VMEM((512, 1024), F32),
            pltpu.VMEM((128, 1024), F32),
            pltpu.VMEM((1040, 1024), BF),
            pltpu.VMEM((1024, 2048), BF),
            pltpu.VMEM((1024, 2048), BF),
            pltpu.SemaphoreType.DMA,
            pltpu.SemaphoreType.DMA((4,)),
        ],
        compiler_params=pltpu.CompilerParams(vmem_limit_bytes=48 * 2**20),
        name="update",
    )(red, modes, members.reshape(1024, 2048))
    return inc, ana.reshape(64, 16, 2048)


def solution(mesh):
    placed = (
        P(None, "band", "tile"),
        P(),
        P(("tile", "band")),
        P(("tile", "band")),
        P(("tile", "band")),
        P(("tile", "band")),
        P(("tile", "band")),
        P(("tile", "band")),
    )
    return jax.shard_map(
        per_device,
        mesh=mesh,
        in_specs=placed,
        out_specs=(P("band", "tile"), P(None, "band", "tile")),
        check_vma=False,
    )
```

time: 558 us -> 102 us (0.18); the launches traced: 551 us -> 101 us
  waiting for transfers between devices: 174 us -> 0.01 us
  other arithmetic: 133 us -> 0 us
  Pallas kernels: 0 us -> 85.7 us
  local copies, waits for them, and re-layouts: 90.1 us -> 8.02 us
  blocking collectives: 80.9 us -> 0 us
  matrix products: 49.3 us -> 0 us
  between operations: 17.5 us -> 0.92 us
    psum x1 -> x0, waiting for transfers between devices: 174 us -> none  [per_device(): gram, cross, drive = lax.psum((gram, cross, drive), ('tile', 'band'))]
    another operation x19 -> x0, other arithmetic: 120 us -> none  [the longest x15 79.3 us: per_device(): lower = jnp.linalg.cholesky(gram + prior)]
    pallas_call x0 -> x4, Pallas kernels: none -> 85.7 us  [the longest x1 36.1 us: per_device(): pl.pallas_call(reduce_kernel, out_shape=jax.ShapeDtypeStruct((ROWS, 128),...]
    psum x1 -> x0, blocking collectives: 80.9 us -> none  [per_device(): gram, cross, drive = lax.psum((gram, cross, drive), ('tile', 'band'))]
    gather x4 -> x0, local copies, waits for them, and re-layouts: 56.2 us -> none  [the longest x2 28.5 us: per_device(): jnp.take(flat, (obs_level + 1 + offset) * cells_dev + obs_cell, axis=1)]
    dot_general x9 -> x0, matrix products: 43.4 us -> none  [the longest x1 13.5 us: per_device(): jnp.einsum('lpk,plc->klc', member_weights, members, preferred_element_typ...]
    concatenate x1 -> x0, local copies, waits for them, and re-layouts: 12.6 us -> none  [padded_2(): jnp.concatenate([lax.ppermute(tail, axis, [(i, (i + 1) % count) for i in...]
    another operation x35 -> x0, local copies, waits for them, and re-layouts: 11.5 us -> none
  transfers between devices with their start and end apart: 3 -> 2, of which waited for: 1 -> 0; matrix products, arithmetic and copies ran while one was open for 2% -> 0% of each run, Pallas kernels for 0% -> 6%
where the time goes in v1:
time: 102 us; the launch traced here: 101 us
  Pallas kernels  85.7 us (84%)
  local copies, waits for them, and re-layouts  8.02 us (8%)
  starting transfers between devices  6.52 us (6%)
    pallas_call x1, Pallas kernels, per_device(): pl.pallas_call(reduce_kernel, out_shape=jax.ShapeDtypeStruct((ROWS, 128),...  36.1 us
    pallas_call x1, Pallas kernels, per_device(): pl.pallas_call(update_kernel, out_shape=(jax.ShapeDtypeStruct((16, 2048),...  27.6 us
    pallas_call x1, Pallas kernels, per_device(): pl.pallas_call(sums_kernel, out_shape=jax.ShapeDtypeStruct((ROWS, 128), F...  15.8 us
    ppermute x2, starting transfers between devices, beside(): return lax.ppermute(a, 'band', pairs)  6.52 us
    pallas_call x1, Pallas kernels, per_device(): pl.pallas_call(scatter_kernel, out_shape=jax.ShapeDtypeStruct((864, 256),...  6.24 us
    unnamed x18, local copies, waits for them, and re-layouts  4.86 us
    slice x1, local copies, waits for them, and re-layouts, per_device(): hi = beside(members[:, 0, :], False)  3.16 us
  transfers between devices with their start and end apart: 2, of which 0 were waited for; matrix products, arithmetic and copies ran while one was open for 0% of the time, Pallas kernels for 6%

profile of v1, /device:TPU:1, one launch (start us, length us, event | category | flops | bytes accessed | tf_op | source)
XLA Modules:
  0.0 101.2 jit_solution(10948580080539238572)
XLA Ops:
  0.6 3.2 %fusion = (bf16[64,1,2048]{2,1,0:T(2,128)(2,1)S(1)}, bf16[64,1,2048]{2,1,0:T(2,128)(2,1)S(1)}) fusion(bf16[64,16,2048]{2,1,0:T(8,128)(2,1)} %mem_ref.1), kind=kLoop, calls=%fused_computation.2 | loop fusion | bytes 1048576 | tf_op jit(solution)/shard_map/slice | solution.py:372
  3.8 0.2 copy.17
  4.0 4.6 %collective-permute-start = (bf16[64,2048]{1,0:T(8,128)(2,1)S(1)}, bf16[64,2048]{1,0:T(8,128)(2,1)S(1)}, u32[]{:S(2)}, u32[]{:S(2)}) collective-permute-start(bf16[64,2048]{1,0:T(8,128)(2,1)S(1)} %bitcast.21), channel_id=1, source_target_pairs={{0,1},{1,2},{2,3},{3,4},{4,5},{5,6},{6,7},{8,9},{9,10},{10,11},{11... | collective-permute-start | bytes 786440 | tf_op jit(solution)/shard_map/ppermute | solution.py:369
  8.6 0.2 copy.16
  8.7 1.9 %collective-permute-start.1 = (bf16[64,2048]{1,0:T(8,128)(2,1)S(1)}, bf16[64,2048]{1,0:T(8,128)(2,1)S(1)}, u32[]{:S(2)}, u32[]{:S(2)}) collective-permute-start(bf16[64,2048]{1,0:T(8,128)(2,1)S(1)} %bitcast.22), channel_id=1, source_target_pairs={{1,0},{2,1},{3,2},{4,3},{5,4},{6,5},{7,6},{9,8},{10,9},{11,10},{12... | collective-permute-start | bytes 786440 | tf_op jit(solution)/shard_map/ppermute | solution.py:369
  10.6 0.0 copy-start.2
  10.7 0.7 copy-done.2
  11.4 0.0 copy-start.3
  11.4 0.8 copy-done.3
  12.2 0.0 copy-start.4
  12.2 0.8 copy-done.4
  12.9 0.0 copy-start.5
  12.9 0.8 copy-done.5
  13.7 0.8 copy-done.6
  14.4 0.8 copy-done.7
  15.2 6.2 %scatter.1.field_ref = f32[864,256]{1,0:T(8,128)S(1)} custom-call(s32[64,128]{1,0:T(8,128)S(1)} %bitcast.15, s32[64,128]{1,0:T(8,128)S(1)} %bitcast.16, s32[64,128]{1,0:T(8,128)S(1)} %bitcast.17, f32[64,128]{1,0:T(8,128)S(1)} %bitcast.18, f32[64,128]{1,0:T(8,128)S(1)} %bitcast.19, f32[64,128]{1,0:T(8,128)S(1)} %bitcast.20), custom_call_target="tpu_custom_call" | custom-call | flops 8000000000 | bytes 1048576 | tf_op jit(solution)/shard_map/scatter/pallas_call | solution.py:374
  21.5 0.0 copy-start
  21.5 0.0 collective-permute-done.lo_ref
  21.5 0.0 collective-permute-done.1.hi_ref
  21.5 0.0 copy-done.1
  21.5 15.8 %sums.1.in_ref = f32[1792,128]{1,0:T(8,128)S(1)} custom-call(f32[864,256]{1,0:T(8,128)S(1)} %scatter.1.field_ref, bf16[64,16,2048]{2,1,0:T(8,128)(2,1)} %mem_ref.1, bf16[64,2048]{1,0:T(8,128)(2,1)S(1)} %collective-permute-done.lo_ref, bf16[64,2048]{1,0:T(8,128)(2,1)S(1)} %collective-permute-done.1.hi_ref, f32[8,128]{1,0:T(8,128)S(1)} %copy-done.1), custom_call_target="tpu_custom_call" | custom-call | tf_op jit(solution)/shard_map/sums/pallas_call | solution.py:384
  37.3 36.1 %reduce.1.red_ref = f32[1792,128]{1,0:T(8,128)S(1)} custom-call(f32[1792,128]{1,0:T(8,128)S(1)} %sums.1.in_ref), custom_call_target="tpu_custom_call" | custom-call | tf_op jit(solution)/shard_map/reduce/pallas_call | solution.py:398
  73.3 0.0 copy-done
  73.4 27.6 %update.1 = (f32[16,2048]{1,0:T(8,128)}, bf16[1024,2048]{1,0:T(8,128)(2,1)}) custom-call(f32[1792,128]{1,0:T(8,128)S(1)} %reduce.1.red_ref, f32[8,128]{1,0:T(8,128)S(1)} %copy-done.1, bf16[1024,2048]{1,0:T(8,128)(2,1)S(1)} %bitcast.14), custom_call_target="tpu_custom_call" | custom-call | tf_op jit(solution)/shard_map/update/pallas_call | solution.py:415
  (3 shorter events, 0.0 us)
Async XLA Ops:
  4.0 17.5 %collective-permute-start = (bf16[64,2048]{1,0:T(8,128)(2,1)S(1)}, bf16[64,2048]{1,0:T(8,128)(2,1)S(1)}, u32[]{:S(2)}, u32[]{:S(2)}) collective-permute-start(bf16[64,2048]{1,0:T(8,128)(2,1)S(1)} %bitcast.21), channel_id=1, source_target_pairs={{0,1},{1,2},{2,3},{3,4},{4,5},{5,6},{6,7},{8,9},{9,10},{10,11},{11... | collective-permute-start | bytes 786440 | tf_op jit(solution)/shard_map/ppermute | solution.py:369
  8.7 12.8 %collective-permute-start.1 = (bf16[64,2048]{1,0:T(8,128)(2,1)S(1)}, bf16[64,2048]{1,0:T(8,128)(2,1)S(1)}, u32[]{:S(2)}, u32[]{:S(2)}) collective-permute-start(bf16[64,2048]{1,0:T(8,128)(2,1)S(1)} %bitcast.22), channel_id=1, source_target_pairs={{1,0},{2,1},{3,2},{4,3},{5,4},{6,5},{7,6},{9,8},{10,9},{11,10},{12... | collective-permute-start | bytes 786440 | tf_op jit(solution)/shard_map/ppermute | solution.py:369
  10.6 0.8 copy-start.2
  11.4 0.8 copy-start.3
  12.2 0.8 copy-start.4
  12.9 0.8 copy-start.5
  13.7 0.8 copy-start.6
  14.4 0.8 copy-start.7
  15.2 6.3 %copy-start.1 = (f32[8,128]{1,0:T(8,128)S(1)}, f32[8,128]{1,0:T(8,128)}, u32[]{:S(2)}) copy-start(f32[8,128]{1,0:T(8,128)} %modes_ref.3) | copy-start | bytes 12292
  21.5 51.9 %copy-start = (bf16[64,16,2048]{2,1,0:T(8,128)(2,1)S(1)}, bf16[64,16,2048]{2,1,0:T(8,128)(2,1)}, u32[]{:S(2)}) copy-start(bf16[64,16,2048]{2,1,0:T(8,128)(2,1)} %mem_ref.1) | copy-start | bytes 12582916

commit v2 on v1

v2 whole, which is shorter than its diff:
```python
import jax
import jax.numpy as jnp
from jax import lax
from jax.experimental import pallas as pl
from jax.experimental.pallas import tpu as pltpu
from jax.sharding import PartitionSpec as P

BF = jnp.bfloat16
F32 = jnp.float32
VM = pl.BlockSpec(memory_space=pltpu.VMEM)
NT = (((1,), (1,)), ((), ()))
STRIDE = 24
ROWS = 1536
HALF = ROWS // 2
PART = HALF // 2
PIECE = PART // 16


def convert(mem_s, x32_s):
    def conv(m, _):
        v = mem_s[pl.ds(pl.multiple_of(m * 16, 16), 16), :].astype(F32)
        for k in range(16):
            x32_s[k, pl.ds(pl.multiple_of(m * STRIDE + 8, 8), 16), :] = v[:, 128 * k : 128 * k + 128]
        return 0
    lax.fori_loop(0, 64, conv, 0, unroll=2)


def scatter(obs_s, first, field_s, lhs_s, hot_s):
    cell_s, level_s, side_s, weight_s, scale_s, innov_s = obs_s
    rows16 = lax.broadcasted_iota(jnp.int32, (16, 128), 0).astype(F32)
    zero = jnp.zeros((16, 128), BF)
    one = jnp.ones((16, 128), BF)

    def split(v):
        hi = v.astype(BF).astype(F32)
        return hi, v - hi

    def fill(i, slot):
        sl = pl.ds(pl.multiple_of(i * 8, 8), 8)
        cell = cell_s[sl, :]
        lev = level_s[sl, :]
        side = side_s[sl, :]
        w = weight_s[sl, :]
        s = scale_s[sl, :]
        ch = cell >> 8
        keys = [
            (cell & 255).astype(F32),
            ((lev + 1) * 8 + ch).astype(F32),
            ((lev + 2 * side) * 8 + ch).astype(F32),
            ((lev + side + 1) * 8 + ch).astype(F32),
        ]
        a = s * (1.0 - w)
        b = s * w
        t = s * innov_s[sl, :]
        vals = [x for v in (a * a, b * b, a * b, a * t, b * t) for x in split(v)]
        for k in range(8):
            cols = slice(128 * k, 128 * k + 128)

            def wide(v):
                return jnp.broadcast_to(v[k : k + 1, :], (16, 128)).astype(BF)

            cl, kn, kf, kp = [wide(v) for v in keys]
            dn0, dn1, df0, df1, e0, e1, gn0, gn1, gf0, gf1 = [wide(v) for v in vals]
            for g in range(10):
                it = (rows16 + 16.0 * g).astype(BF)
                at = 16 * g
                if g < 9:
                    mn = it == kn
                    mf = it == kf
                    lhs_s[slot, pl.ds(at, 16), cols] = jnp.where(mn, dn0, jnp.where(mf, df0, zero))
                    lhs_s[slot, pl.ds(144 + at, 16), cols] = jnp.where(mn, dn1, jnp.where(mf, df1, zero))
                    lhs_s[slot, pl.ds(288 + at, 16), cols] = jnp.where(mn, gn0, jnp.where(mf, gf0, zero))
                    lhs_s[slot, pl.ds(432 + at, 16), cols] = jnp.where(mn, gn1, jnp.where(mf, gf1, zero))
                mp = it == kp
                lhs_s[slot, pl.ds(576 + at, 16), cols] = jnp.where(mp, e0, zero)
                lhs_s[slot, pl.ds(736 + at, 16), cols] = jnp.where(mp, e1, zero)
            for g in range(16):
                it = (rows16 + 16.0 * g).astype(BF)
                hot_s[slot, pl.ds(16 * g, 16), cols] = jnp.where(it == cl, one, zero)

    def add(slot):
        field_s[...] += lax.dot_general(lhs_s[slot], hot_s[slot], NT, preferred_element_type=F32)

    fill(first, 0)

    def steps(i, _):
        at = first + 2 * i
        fill(at + 1, 1)
        add(0)
        fill(at + 2, 0)
        add(1)
        return 0

    lax.fori_loop(0, 1, steps, 0)
    fill(first + 3, 1)
    add(0)
    add(1)


def products(field_s, x32_s, stack_s, prod_s):
    first = lax.broadcasted_iota(jnp.int32, (16, 128), 0)
    lane = lax.broadcasted_iota(jnp.int32, (144, 128), 1)

    def field(base, step, r):
        at = pl.multiple_of(base + 8 * r, 8)
        return field_s[pl.ds(at, 8), :] + field_s[pl.ds(pl.multiple_of(at + step, 8), 8), :]

    def fill(q, slot):
        r = 2 * q
        below = jnp.maximum(r - 1, 0)
        ed = [field(576, 160, r + i) for i in range(2)]
        dd = [field(0, 144, r + i) for i in range(2)]
        gd = [field(288, 144, r + i) for i in range(2)]
        for k in range(16):
            cs = slice(128 * k, 128 * k + 128)

            def row(v):
                return v[k // 2 : k // 2 + 1, 128 * (k % 2) : 128 * (k % 2) + 128]

            xs = [x32_s[k, pl.ds(7 + l, 64, stride=STRIDE), :] for l in (below, r, r + 1)]
            for h in range(2):
                base = 144 * h
                stack_s[slot, pl.ds(288 + 64 * h, 64), cs] = xs[h + 1].astype(BF)
                stack_s[slot, pl.ds(base, 64), cs] = (xs[h + 1] * row(dd[h])).astype(BF)
                stack_s[slot, pl.ds(base + 64, 64), cs] = (xs[h] * row(ed[h])).astype(BF)
                g = jnp.broadcast_to(row(gd[h]), (16, 128))
                gh = g.astype(BF).astype(F32)
                both = jnp.where(first == 0, gh, jnp.where(first == 1, g - gh, 0.0))
                stack_s[slot, pl.ds(base + 128, 16), cs] = both.astype(BF)

    def multiply(q, slot):
        p = lax.dot_general(
            stack_s[slot, pl.ds(0, 288), :], stack_s[slot, pl.ds(288, 128), :], NT, preferred_element_type=F32
        )
        prod_s[q] = jnp.where(lane < 64, p[:144], p[144:])

    fill(0, 0)

    def steps(i, _):
        fill(2 * i + 1, 1)
        multiply(2 * i, 0)
        fill(2 * i + 2, 0)
        multiply(2 * i + 1, 1)
        return 0

    lax.fori_loop(0, 4, steps, 0)
    multiply(8, 0)


def coefs(modes_ref, start, coef_s):
    half = lax.broadcasted_iota(jnp.int32, (1, 128), 1) < 64
    for j in range(9):
        if j < 8:
            phi = []
            for r in range(-1, 19):
                l = start + r
                ok = (l >= 0) & (l < 128)
                phi.append(jnp.where(ok, modes_ref[j, jnp.clip(l, 0, 127)], 0.0))
        else:
            phi = [jnp.float32(1.0)] * 20
        for q in range(9):
            for s in range(3):
                r = 2 * q + (1, 0, 2)[s]
                coef_s[s, j, pl.ds(q, 1), :] = jnp.where(half, phi[r], phi[r + 1])


HALVES = [(j, jj) for j in range(8) for jj in range(j, 9)]


def expand(prod_s, above_s, coef_s, out_ref):
    left64 = lax.broadcasted_iota(jnp.int32, (64, 128), 1) < 64

    def transpose(q, _):
        above = jnp.minimum(q + 1, 8)
        t = jnp.concatenate([prod_s[q, pl.ds(64, 64), :], prod_s[above, pl.ds(64, 64), :]], axis=0).T
        right = jnp.where(q < 8, t[:64], 0.0)
        above_s[q] = jnp.where(left64, t[64:], right)
        return 0

    lax.fori_loop(0, 9, transpose, 0)
    lane8 = lax.broadcasted_iota(jnp.int32, (8, 128), 1) < 64

    def group(i, _):
        at = pl.multiple_of(i * 8, 8)
        s0 = [prod_s[q, pl.ds(at, 8), :] for q in range(9)]
        s1 = [prod_s[q, pl.ds(pl.multiple_of(64 + at, 8), 8), :] for q in range(9)]
        s2 = [above_s[q, pl.ds(at, 8), :] for q in range(9)]
        held, t = None, None
        for n, (j, jj) in enumerate(HALVES):
            if jj == j:
                t = [
                    s0[q] * coef_s[0, j, pl.ds(q, 1), :]
                    + s1[q] * coef_s[1, j, pl.ds(q, 1), :]
                    + s2[q] * coef_s[2, j, pl.ds(q, 1), :]
                    for q in range(9)
                ]
            acc = t[0] * coef_s[0, jj, pl.ds(0, 1), :]
            for q in range(1, 9):
                acc = acc + t[q] * coef_s[0, jj, pl.ds(q, 1), :]
            acc = acc + pltpu.roll(acc, 64, 1)
            if n % 2 == 0:
                held = acc
            else:
                out_ref[pl.ds(pl.multiple_of(n // 2 * 64 + at, 8), 8), :] = jnp.where(lane8, held, acc)
        return 0

    lax.fori_loop(0, 8, group, 0)
    out_ref[pl.ds(1408, 128), :] = jnp.zeros((128, 128), F32)
    for j in range(8):
        dr = jnp.zeros((1, 128), F32)
        for q in range(9):
            g = prod_s[q, pl.ds(128, 8), :]
            dr = dr + (g[0:1] + g[1:2]) * coef_s[0, j, pl.ds(q, 1), :]
        out_ref[pl.ds(1408 + j, 1), :] = dr + pltpu.roll(dr, 64, 1)


def front_kernel(
    cell_h, level_h, side_h, weight_h, scale_h, innov_h, mem_h, modes_ref, out_ref,
    cell_s, level_s, side_s, weight_s, scale_s, innov_s, mem_s, lhs_s, hot_s, field_s, x32_s, stack_s, prod_s, above_s,
    coef_s, edge_s, halo_s, part_s, from_core, acc_s, from_plane, from_line,
    obs_sem, mem_sem, send0, recv0, send1, recv1, send2, recv2, send3, recv3, send4, recv4, send5, recv5,
):
    tile = lax.axis_index("tile")
    band = lax.axis_index("band")
    x, z, y, core = tile // 8, tile % 8, band // 2, band % 2

    def dev(xx, yy, zz, cc):
        return (xx * 8 + zz, yy * 2 + cc)

    def plane(e):
        return (x + e // 4) % 4, (y + e % 4) % 4

    order = sorted(range(1, 16), key=lambda e: -(min(e // 4, 4 - e // 4) + min(e % 4, 4 - e % 4)))
    sibling = dev(x, y, z, 1 - core)
    up = (tile, (band + 1) % 8)
    down = (tile, (band + 7) % 8)
    partners = [up, down]
    for e in range(1, 16):
        partners.append(dev(*plane(e), z, core))
    for e in range(1, 8):
        partners.append(dev(x, y, (z + e) % 8, core))
    barrier = pltpu.get_barrier_semaphore()
    for d in partners:
        pl.semaphore_signal(barrier, inc=1, device_id=d, device_id_type=pl.DeviceIdType.MESH)

    obs_s = (cell_s, level_s, side_s, weight_s, scale_s, innov_s)
    loads = []
    for n, (h, s) in enumerate(zip((cell_h, level_h, side_h, weight_h, scale_h, innov_h), obs_s)):
        c = pltpu.make_async_copy(h, s, obs_sem.at[n])
        c.start()
        loads.append(c)
    mem_load = pltpu.make_async_copy(mem_h, mem_s, mem_sem)
    mem_load.start()
    coefs(modes_ref, band * 16 - 1, coef_s)
    field_s[...] = jnp.zeros_like(field_s)
    for c in loads:
        c.wait()
    scatter(obs_s, 0, field_s, lhs_s, hot_s)
    mem_load.wait()
    convert(mem_s, x32_s)
    for k in range(16):
        cs = slice(128 * k, 128 * k + 128)
        edge_s[0, :, cs] = x32_s[k, pl.ds(8, 64, stride=STRIDE), :].astype(BF)
        edge_s[1, :, cs] = x32_s[k, pl.ds(23, 64, stride=STRIDE), :].astype(BF)
    pl.semaphore_wait(barrier, len(partners))

    def copy(src, dst, ss, rs, d):
        c = pltpu.make_async_remote_copy(
            src_ref=src, dst_ref=dst, send_sem=ss, recv_sem=rs, device_id=d, device_id_type=pl.DeviceIdType.MESH
        )
        c.start()
        return c

    halo = [
        copy(edge_s.at[0], halo_s.at[1], send0.at[0], recv0.at[0], down),
        copy(edge_s.at[1], halo_s.at[0], send0.at[1], recv0.at[1], up),
    ]
    scatter(obs_s, 4, field_s, lhs_s, hot_s)
    for c in halo:
        c.wait()
    for k in range(16):
        cs = slice(128 * k, 128 * k + 128)
        x32_s[k, pl.ds(7, 64, stride=STRIDE), :] = jnp.where(band > 0, halo_s[0, :, cs].astype(F32), 0.0)
        x32_s[k, pl.ds(24, 64, stride=STRIDE), :] = jnp.where(band < 7, halo_s[1, :, cs].astype(F32), 0.0)
    products(field_s, x32_s, stack_s, prod_s)
    expand(prod_s, above_s, coef_s, part_s)

    mine = core * HALF
    other = (1 - core) * HALF
    place = x * 4 + y

    def rows(base, at, n):
        return pl.ds(pl.multiple_of(base + at, 8), n)

    step1, step2, step3, step4, step5 = [], [], [], [], []
    for i in range(2):
        step1.append(
            copy(part_s.at[rows(other, i * PART, PART)], from_core.at[pl.ds(i * PART, PART)], send1.at[i], recv1.at[i], sibling)
        )
    for i in range(2):
        step1[i].wait_recv()
        acc_s[pl.ds(i * PART, PART), :] = part_s[rows(mine, i * PART, PART), :] + from_core[pl.ds(i * PART, PART), :]
        for e in order:
            xx, yy = plane(e)
            src = acc_s.at[rows((xx * 4 + yy) * PIECE, i * PART, PIECE)]
            step2.append(copy(src, from_plane.at[i, e], send2.at[i, e], recv2.at[i, e], dev(xx, yy, z, core)))
    for i in range(2):
        total = acc_s[rows(place * PIECE, i * PART, PIECE), :]
        for n, e in enumerate(order):
            step2[15 * i + n].wait_recv()
            total = total + from_plane[i, e]
        from_line[i, z] = total
        for e in (4, 3, 5, 2, 6, 1, 7):
            ref = from_line.at[i, z]
            step3.append(copy(ref, ref, send3.at[i, e], recv3.at[i, e], dev(x, y, (z + e) % 8, core)))
    for i in range(2):
        for c in step3[7 * i : 7 * i + 7]:
            c.wait_recv()
        total = from_line[i, 0]
        for e in range(1, 8):
            total = total + from_line[i, e]
        at = rows(mine, i * PART + place * PIECE, PIECE)
        out_ref[at, :] = total
        ref = out_ref.at[at]
        for e in order:
            step4.append(copy(ref, ref, send4.at[i, e], recv4.at[i, e], dev(*plane(e), z, core)))
        step5.append(copy(ref, ref, send5.at[i, 0], recv5.at[i, 0], sibling))
    for i in range(2):
        for n, e in reversed(list(enumerate(order))):
            step4[15 * i + n].wait_recv()
            xx, yy = (x + 4 - e // 4) % 4, (y + 4 - e % 4) % 4
            ref = out_ref.at[rows(mine, i * PART + (xx * 4 + yy) * PIECE, PIECE)]
            step5.append(copy(ref, ref, send5.at[i, e], recv5.at[i, e], sibling))
    for c in step5:
        c.wait_recv()
    for c in step1 + step2 + step3 + step4 + step5:
        c.wait_send()


def dot(a, b, dims=(((1,), (0,)), ((), ()))):
    return lax.dot_general(a, b, dims, precision=lax.Precision.HIGHEST, preferred_element_type=F32)


def invert(m):
    lane = lax.broadcasted_iota(jnp.int32, (8, 128), 1)
    sub = lax.broadcasted_iota(jnp.int32, (8, 128), 0)
    def col(v, c):
        return jnp.broadcast_to(v[:, c:c + 1], (8, 128))
    def rowb(v, c):
        return jnp.broadcast_to(v[c:c + 1, :], (8, 128))
    for p in range(16):
        b = m[p]
        v = [col(b, 8 * p + c) for c in range(8)]
        for c in range(8):
            d = 1.0 / rowb(v[c], c)
            here = sub == c
            for e in range(c + 1, 8):
                r = rowb(v[e], c)
                v[e] = jnp.where(here, v[e] * d, v[e] - (v[c] * r) * d)
            at = lane == 8 * p + c
            r = jnp.where(at, 1.0, rowb(b, c)) * d
            b = jnp.where(here, r, jnp.where(at, 0.0, b) - v[c] * r)
        rows = [rowb(b, c) for c in range(8)]
        panel = (lane >= 8 * p) & (lane < 8 * p + 8)
        order = [i % 16 for i in range(p + 1, p + 16)]
        new = list(m)
        new[p] = b
        for i in order:
            terms = [col(m[i], 8 * p + c) * rows[c] for c in range(8)]
            while len(terms) > 1:
                terms = [x + y for x, y in zip(terms[::2], terms[1::2])]
            new[i] = jnp.where(panel, 0.0, m[i]) - terms[0]
        m = new
    return m

def solve(red_ref, a_s, w_s):
    lane = lax.broadcasted_iota(jnp.int32, (64, 128), 1)
    sub = lax.broadcasted_iota(jnp.int32, (64, 128), 0)
    where = {pair: n for n, pair in enumerate(HALVES)}

    def half(j, jj, side):
        n = where[j, jj]
        v = red_ref[pl.ds(64 * (n // 2), 64), :]
        return v if n % 2 == side else pltpu.roll(v, 64, 1)

    for j in range(8):
        for pair in range(j // 2, 5):
            if pair == 4:
                r = jnp.broadcast_to(red_ref[pl.ds(1408 + j, 1), :], (64, 128))
                drive = jnp.sum(jnp.where(lane == sub, r, 0.0), axis=1, keepdims=True)
                u = jnp.where(lane < 64, half(j, 8, 0), jnp.where(lane == 64, drive, 0.0))
            elif 2 * pair < j:
                t = a_s[pl.ds(64 * j - 64, 64), pl.ds(128 * pair, 128)]
                t = jnp.concatenate([t, t], axis=0).T[64:]
                u = jnp.where(lane < 64, t, half(j, j, 1))
            else:
                u = jnp.where(lane < 64, half(j, 2 * pair, 0), half(j, 2 * pair + 1, 1))
            if pair == j // 2:
                u = jnp.where(lane == sub + 64 * (j % 2), u + 511.0, u)
            a_s[pl.ds(64 * j, 64), pl.ds(128 * pair, 128)] = u
    for k in range(4):
        at = 128 * k
        m = [a_s[pl.ds(at + 8 * i, 8), pl.ds(at, 128)] for i in range(16)]
        inv = jnp.concatenate(invert(m), axis=0)
        w = dot(inv, a_s[pl.ds(at, 128), pl.ds(at + 128, 512 - at)])
        w_s[pl.ds(at, 128), pl.ds(at + 128, 512 - at)] = w
        for i in range(k + 1, 4):
            ki = a_s[pl.ds(at, 128), pl.ds(128 * i, 128)]
            a_s[pl.ds(128 * i, 128), pl.ds(128 * i, 640 - 128 * i)] -= dot(
                ki, w[:, 128 * (i - k - 1):], (((0,), (0,)), ((), ())))
    for k in (2, 1, 0):
        at = 128 * k
        w_s[pl.ds(at, 128), pl.ds(512, 128)] -= dot(
            w_s[pl.ds(at, 128), pl.ds(at + 128, 384 - at)], w_s[pl.ds(at + 128, 384 - at), pl.ds(512, 128)])


def update_kernel(red_ref, modes_ref, mem_hbm, inc_ref, ana_hbm, a_s, w_s, phi_s, u_s, big_s, mem_s, ana_s, load_sem, save_sem):
    load = pltpu.make_async_copy(mem_hbm, mem_s, load_sem)
    load.start()
    solve(red_ref, a_s, w_s)
    shift = lax.rem(128 - lax.axis_index("band") * 16, 128)
    phi = pltpu.roll(modes_ref[...], shift, 1)
    lane = lax.broadcasted_iota(jnp.int32, (8, 128), 1)
    for width in (16, 32, 64):
        phi = jnp.where(lane < width, phi, jnp.where(lane < 2 * width, pltpu.roll(phi, width, 1), 0.0))
    member = lax.broadcasted_iota(jnp.int32, (64, 1024), 0)
    owner = lax.broadcasted_iota(jnp.int32, (64, 1024), 1) // 16
    for j in range(8):
        wide = jnp.concatenate([jnp.broadcast_to(phi[j : j + 1, :], (64, 128))] * 8, axis=1)
        phi_s[pl.ds(64 * j, 64), :] = jnp.where(member == owner, wide, 0.0)
    u_s[...] = dot(w_s[:, 512:640], phi_s[...], (((0,), (0,)), ((), ())))
    level = lax.broadcasted_iota(jnp.int32, (16, 1024), 1) % 16
    own = level == lax.broadcasted_iota(jnp.int32, (16, 1024), 0)

    def spread(k, _):
        row = jnp.broadcast_to(u_s[pl.ds(k, 1), :], (16, 1024))
        big_s[pl.ds(pl.multiple_of(k * 16, 16), 16), :] = jnp.where(own, row, 0.0).astype(BF)
        return 0

    lax.fori_loop(0, 65, spread, 0, unroll=5)
    load.wait()
    saves = []
    for i in range(4):
        cols = pl.ds(512 * i, 512)
        m = mem_s[:, cols]
        r = jnp.dot(big_s[...], m, preferred_element_type=F32)
        ana_s[:, cols] = (m.astype(F32) - r[:1024]).astype(BF)
        inc_ref[:, cols] = r[1024:]
        save = pltpu.make_async_copy(ana_s.at[:, cols], ana_hbm.at[:, cols], save_sem.at[i])
        save.start()
        saves.append(save)
    for save in saves:
        save.wait()


def per_device(members, modes, *obs):
    flat = members.reshape(1024, 2048)
    anywhere = pl.BlockSpec(memory_space=pl.ANY)
    red = pl.pallas_call(
        front_kernel,
        out_shape=jax.ShapeDtypeStruct((ROWS, 128), F32),
        in_specs=[anywhere] * 7 + [pl.BlockSpec(memory_space=pltpu.SMEM)],
        out_specs=VM,
        scratch_shapes=[pltpu.VMEM((64, 128), jnp.int32)] * 3
        + [pltpu.VMEM((64, 128), F32)] * 3
        + [
            pltpu.VMEM((1024, 2048), BF),
            pltpu.VMEM((2, 896, 1024), BF),
            pltpu.VMEM((2, 256, 1024), BF),
            pltpu.VMEM((896, 256), F32),
            pltpu.VMEM((16, 64 * STRIDE + 8, 128), F32),
            pltpu.VMEM((2, 416, 2048), BF),
            pltpu.VMEM((9, 144, 128), F32),
            pltpu.VMEM((9, 64, 128), F32),
            pltpu.VMEM((3, 9, 9, 128), F32),
            pltpu.VMEM((2, 64, 2048), BF),
            pltpu.VMEM((2, 64, 2048), BF),
            pltpu.VMEM((ROWS, 128), F32),
            pltpu.VMEM((HALF, 128), F32),
            pltpu.VMEM((HALF, 128), F32),
            pltpu.VMEM((2, 16, PIECE, 128), F32),
            pltpu.VMEM((2, 8, PIECE, 128), F32),
            pltpu.SemaphoreType.DMA((6,)),
            pltpu.SemaphoreType.DMA,
        ]
        + [pltpu.SemaphoreType.DMA(n) for n in ((2,), (2,), (2,), (2,))]
        + [pltpu.SemaphoreType.DMA((2, n)) for n in (16, 16, 8, 8, 16, 16, 16, 16)],
        compiler_params=pltpu.CompilerParams(
            collective_id=0, has_side_effects=True, vmem_limit_bytes=56 * 2**20
        ),
        name="front",
    )(*[o.reshape(64, 128) for o in obs], flat, modes)
    inc, ana = pl.pallas_call(
        update_kernel,
        out_shape=(jax.ShapeDtypeStruct((16, 2048), F32), jax.ShapeDtypeStruct((1024, 2048), BF)),
        in_specs=[VM, VM, anywhere],
        out_specs=(VM, anywhere),
        scratch_shapes=[
            pltpu.VMEM((512, 640), F32),
            pltpu.VMEM((512, 640), F32),
            pltpu.VMEM((512, 1024), F32),
            pltpu.VMEM((128, 1024), F32),
            pltpu.VMEM((1040, 1024), BF),
            pltpu.VMEM((1024, 2048), BF),
            pltpu.VMEM((1024, 2048), BF),
            pltpu.SemaphoreType.DMA,
            pltpu.SemaphoreType.DMA((4,)),
        ],
        compiler_params=pltpu.CompilerParams(vmem_limit_bytes=48 * 2**20),
        name="update",
    )(red, modes, flat)
    return inc, ana.reshape(64, 16, 2048)


def solution(mesh):
    placed = (
        P(None, "band", "tile"),
        P(),
        P(("tile", "band")),
        P(("tile", "band")),
        P(("tile", "band")),
        P(("tile", "band")),
        P(("tile", "band")),
        P(("tile", "band")),
    )
    return jax.shard_map(
        per_device,
        mesh=mesh,
        in_specs=placed,
        out_specs=(P("band", "tile"), P(None, "band", "tile")),
        check_vma=False,
    )
```

time: 102 us -> 83.2 us (0.82)
  local copies, waits for them, and re-layouts: 8.02 us -> 1.13 us
  starting transfers between devices: 6.52 us -> 0 us
  Pallas kernels: 85.7 us -> 81 us
    ppermute x2 -> x0, starting transfers between devices: 6.52 us -> none  [beside(): return lax.ppermute(a, 'band', pairs)]
    pallas_call x3 -> x1, Pallas kernels: 58.1 us -> 53.1 us  [per_device(): pl.pallas_call(front_kernel, out_shape=jax.ShapeDtypeStruct((ROWS, 128),...]
    unnamed x18 -> x6, local copies, waits for them, and re-layouts: 4.86 us -> 1.13 us
    slice x1 -> x0, local copies, waits for them, and re-layouts: 3.16 us -> none  [per_device(): hi = beside(members[:, 0, :], False)]
  transfers between devices with their start and end apart: 2 -> 0, of which waited for: 0 -> 0; matrix products, arithmetic and copies ran while one was open for 0% -> 0% of each run, Pallas kernels for 6% -> 0%
where the time goes in v2:
time: 83.2 us; the launch traced here: 83 us
  Pallas kernels  81 us (97%)
  local copies, waits for them, and re-layouts  1.13 us (1%)
  between operations  0.86 us (1%)
    pallas_call x1, Pallas kernels, per_device(): pl.pallas_call(front_kernel, out_shape=jax.ShapeDtypeStruct((ROWS, 128),...  53.1 us
    pallas_call x1, Pallas kernels, per_device(): pl.pallas_call(update_kernel, out_shape=(jax.ShapeDtypeStruct((16, 2048),...  27.9 us

profile of v2, /device:TPU:1, one launch (start us, length us, event | category | flops | bytes accessed | tf_op | source)
XLA Modules:
  0.0 83.0 jit_solution(15259876387112539321)
XLA Ops:
  0.6 0.0 copy-start.2
  0.6 0.0 copy-start
  0.7 53.1 %front.1.red_ref = f32[1536,128]{1,0:T(8,128)} custom-call(s32[64,128]{1,0:T(8,128)} %bitcast.10, s32[64,128]{1,0:T(8,128)} %bitcast.11, s32[64,128]{1,0:T(8,128)} %bitcast.12, f32[64,128]{1,0:T(8,128)} %bitcast.13, f32[64,128]{1,0:T(8,128)} %bitcast.14, f32[64,128]{1,0:T(8,128)} %bitcast.15, bf16[1024,2048]{1,0:T(8,128)(2,1)} %bitcast.8, f32[8,128]{1,0:T(8,128)} %modes_ref.3), custom_call_target="tpu_custom_call" | custom-call | tf_op jit(solution)/shard_map/front/pallas_call | solution.py:459
  53.8 0.0 copy-done.2
  53.8 0.0 copy-done
  53.8 0.0 copy-start.1
  53.8 1.1 %copy-done.1 = f32[1536,128]{1,0:T(8,128)S(1)} copy-done((f32[1536,128]{1,0:T(8,128)S(1)}, f32[1536,128]{1,0:T(8,128)}, u32[]{:S(2)}) %copy-start.1) | copy-done | bytes 786456
  55.0 27.9 %update.1 = (f32[16,2048]{1,0:T(8,128)}, bf16[1024,2048]{1,0:T(8,128)(2,1)}) custom-call(f32[1536,128]{1,0:T(8,128)S(1)} %copy-done.1, f32[8,128]{1,0:T(8,128)S(1)} %copy-done.2, bf16[1024,2048]{1,0:T(8,128)(2,1)S(1)} %bitcast.9), custom_call_target="tpu_custom_call" | custom-call | tf_op jit(solution)/shard_map/update/pallas_call | solution.py:493
Async XLA Ops:
  0.6 53.2 %copy-start.2 = (f32[8,128]{1,0:T(8,128)S(1)}, f32[8,128]{1,0:T(8,128)}, u32[]{:S(2)}) copy-start(f32[8,128]{1,0:T(8,128)} %modes_ref.3) | copy-start | bytes 12292
  0.6 53.2 %copy-start = (bf16[64,16,2048]{2,1,0:T(8,128)(2,1)S(1)}, bf16[64,16,2048]{2,1,0:T(8,128)(2,1)}, u32[]{:S(2)}) copy-start(bf16[64,16,2048]{2,1,0:T(8,128)(2,1)} %param.8) | copy-start | bytes 12582916
  53.8 1.1 %copy-start.1 = (f32[1536,128]{1,0:T(8,128)S(1)}, f32[1536,128]{1,0:T(8,128)}, u32[]{:S(2)}) copy-start(f32[1536,128]{1,0:T(8,128)} %front.1.red_ref) | copy-start | bytes 2359300

commit v3 on v2

--- a/solution.py
+++ b/solution.py
@@ -11,8 +11,7 @@
 NT = (((1,), (1,)), ((), ()))
 STRIDE = 24
 ROWS = 1536
-HALF = ROWS // 2
-PART = HALF // 2
+PART = ROWS // 4
 PIECE = PART // 16
 
 
@@ -25,7 +24,7 @@
     lax.fori_loop(0, 64, conv, 0, unroll=2)
 
 
-def scatter(obs_s, first, field_s, lhs_s, hot_s):
+def scatter(obs_s, field_s, lhs_s, hot_s):
     cell_s, level_s, side_s, weight_s, scale_s, innov_s = obs_s
     rows16 = lax.broadcasted_iota(jnp.int32, (16, 128), 0).astype(F32)
     zero = jnp.zeros((16, 128), BF)
@@ -81,23 +80,22 @@
     def add(slot):
         field_s[...] += lax.dot_general(lhs_s[slot], hot_s[slot], NT, preferred_element_type=F32)
 
-    fill(first, 0)
+    fill(0, 0)
 
     def steps(i, _):
-        at = first + 2 * i
-        fill(at + 1, 1)
+        fill(2 * i + 1, 1)
         add(0)
-        fill(at + 2, 0)
+        fill(2 * i + 2, 0)
         add(1)
         return 0
 
-    lax.fori_loop(0, 1, steps, 0)
-    fill(first + 3, 1)
+    lax.fori_loop(0, 3, steps, 0)
+    fill(7, 1)
     add(0)
     add(1)
 
 
-def products(field_s, x32_s, stack_s, prod_s):
+def products(ends, field_s, x32_s, stack_s, prod_s):
     first = lax.broadcasted_iota(jnp.int32, (16, 128), 0)
     lane = lax.broadcasted_iota(jnp.int32, (144, 128), 1)
 
@@ -134,17 +132,22 @@
         )
         prod_s[q] = jnp.where(lane < 64, p[:144], p[144:])
 
+    fill(1, 0)
+
+    def steps(i, _):
+        fill(2 * i + 2, 1)
+        multiply(2 * i + 1, 0)
+        fill(2 * i + 3, 0)
+        multiply(2 * i + 2, 1)
+        return 0
+
+    lax.fori_loop(0, 3, steps, 0)
+    multiply(7, 0)
+    ends()
     fill(0, 0)
-
-    def steps(i, _):
-        fill(2 * i + 1, 1)
-        multiply(2 * i, 0)
-        fill(2 * i + 2, 0)
-        multiply(2 * i + 1, 1)
-        return 0
-
-    lax.fori_loop(0, 4, steps, 0)
-    multiply(8, 0)
+    fill(8, 1)
+    multiply(0, 0)
+    multiply(8, 1)
 
 
 def coefs(modes_ref, start, coef_s):
@@ -167,7 +170,7 @@
 HALVES = [(j, jj) for j in range(8) for jj in range(j, 9)]
 
 
-def expand(prod_s, above_s, coef_s, out_ref):
+def levels_above(prod_s, above_s):
     left64 = lax.broadcasted_iota(jnp.int32, (64, 128), 1) < 64
 
     def transpose(q, _):
@@ -178,10 +181,14 @@
         return 0
 
     lax.fori_loop(0, 9, transpose, 0)
+
+
+def expand(part, prod_s, above_s, coef_s, out_ref):
+    base = part * 768
     lane8 = lax.broadcasted_iota(jnp.int32, (8, 128), 1) < 64
 
     def group(i, _):
-        at = pl.multiple_of(i * 8, 8)
+        at = pl.multiple_of(part * 32 + i * 8, 8)
         s0 = [prod_s[q, pl.ds(at, 8), :] for q in range(9)]
         s1 = [prod_s[q, pl.ds(pl.multiple_of(64 + at, 8), 8), :] for q in range(9)]
         s2 = [above_s[q, pl.ds(at, 8), :] for q in range(9)]
@@ -201,17 +208,19 @@
             if n % 2 == 0:
                 held = acc
             else:
-                out_ref[pl.ds(pl.multiple_of(n // 2 * 64 + at, 8), 8), :] = jnp.where(lane8, held, acc)
+                out_ref[pl.ds(pl.multiple_of(base + n // 2 * 32 + i * 8, 8), 8), :] = jnp.where(lane8, held, acc)
         return 0
 
-    lax.fori_loop(0, 8, group, 0)
-    out_ref[pl.ds(1408, 128), :] = jnp.zeros((128, 128), F32)
+    lax.fori_loop(0, 4, group, 0)
+    out_ref[pl.ds(base + 704, 64), :] = jnp.zeros((64, 128), F32)
+    if part > 0:
+        return
     for j in range(8):
         dr = jnp.zeros((1, 128), F32)
         for q in range(9):
             g = prod_s[q, pl.ds(128, 8), :]
             dr = dr + (g[0:1] + g[1:2]) * coef_s[0, j, pl.ds(q, 1), :]
-        out_ref[pl.ds(1408 + j, 1), :] = dr + pltpu.roll(dr, 64, 1)
+        out_ref[pl.ds(704 + j, 1), :] = dr + pltpu.roll(dr, 64, 1)
 
 
 def front_kernel(
@@ -255,7 +264,7 @@
     field_s[...] = jnp.zeros_like(field_s)
     for c in loads:
         c.wait()
-    scatter(obs_s, 0, field_s, lhs_s, hot_s)
+    scatter(obs_s, field_s, lhs_s, hot_s)
     mem_load.wait()
     convert(mem_s, x32_s)
     for k in range(16):
@@ -275,37 +284,36 @@
         copy(edge_s.at[0], halo_s.at[1], send0.at[0], recv0.at[0], down),
         copy(edge_s.at[1], halo_s.at[0], send0.at[1], recv0.at[1], up),
     ]
-    scatter(obs_s, 4, field_s, lhs_s, hot_s)
-    for c in halo:
-        c.wait()
-    for k in range(16):
-        cs = slice(128 * k, 128 * k + 128)
-        x32_s[k, pl.ds(7, 64, stride=STRIDE), :] = jnp.where(band > 0, halo_s[0, :, cs].astype(F32), 0.0)
-        x32_s[k, pl.ds(24, 64, stride=STRIDE), :] = jnp.where(band < 7, halo_s[1, :, cs].astype(F32), 0.0)
-    products(field_s, x32_s, stack_s, prod_s)
-    expand(prod_s, above_s, coef_s, part_s)
-
-    mine = core * HALF
-    other = (1 - core) * HALF
+    def ends():
+        for c in halo:
+            c.wait()
+        for k in range(16):
+            cs = slice(128 * k, 128 * k + 128)
+            x32_s[k, pl.ds(7, 64, stride=STRIDE), :] = jnp.where(band > 0, halo_s[0, :, cs].astype(F32), 0.0)
+            x32_s[k, pl.ds(24, 64, stride=STRIDE), :] = jnp.where(band < 7, halo_s[1, :, cs].astype(F32), 0.0)
+
+    products(ends, field_s, x32_s, stack_s, prod_s)
+
     place = x * 4 + y
 
-    def rows(base, at, n):
-        return pl.ds(pl.multiple_of(base + at, 8), n)
+    def rows(i, whose, at, n):
+        return pl.ds(pl.multiple_of((2 * i + whose) * PART + at, 8), n)
 
     step1, step2, step3, step4, step5 = [], [], [], [], []
+    levels_above(prod_s, above_s)
     for i in range(2):
-        step1.append(
-            copy(part_s.at[rows(other, i * PART, PART)], from_core.at[pl.ds(i * PART, PART)], send1.at[i], recv1.at[i], sibling)
-        )
+        expand(i, prod_s, above_s, coef_s, part_s)
+        ref = part_s.at[rows(i, 1 - core, 0, PART)]
+        step1.append(copy(ref, from_core.at[i], send1.at[i], recv1.at[i], sibling))
     for i in range(2):
         step1[i].wait_recv()
-        acc_s[pl.ds(i * PART, PART), :] = part_s[rows(mine, i * PART, PART), :] + from_core[pl.ds(i * PART, PART), :]
+        acc_s[i] = part_s[rows(i, core, 0, PART), :] + from_core[i]
         for e in order:
             xx, yy = plane(e)
-            src = acc_s.at[rows((xx * 4 + yy) * PIECE, i * PART, PIECE)]
+            src = acc_s.at[i, pl.ds(pl.multiple_of((xx * 4 + yy) * PIECE, 8), PIECE)]
             step2.append(copy(src, from_plane.at[i, e], send2.at[i, e], recv2.at[i, e], dev(xx, yy, z, core)))
     for i in range(2):
-        total = acc_s[rows(place * PIECE, i * PART, PIECE), :]
+        total = acc_s[i, pl.ds(pl.multiple_of(place * PIECE, 8), PIECE), :]
         for n, e in enumerate(order):
             step2[15 * i + n].wait_recv()
             total = total + from_plane[i, e]
@@ -319,7 +327,7 @@
         total = from_line[i, 0]
         for e in range(1, 8):
             total = total + from_line[i, e]
-        at = rows(mine, i * PART + place * PIECE, PIECE)
+        at = rows(i, core, place * PIECE, PIECE)
         out_ref[at, :] = total
         ref = out_ref.at[at]
         for e in order:
@@ -329,7 +337,7 @@
         for n, e in reversed(list(enumerate(order))):
             step4[15 * i + n].wait_recv()
             xx, yy = (x + 4 - e // 4) % 4, (y + 4 - e % 4) % 4
-            ref = out_ref.at[rows(mine, i * PART + (xx * 4 + yy) * PIECE, PIECE)]
+            ref = out_ref.at[rows(i, core, (xx * 4 + yy) * PIECE, PIECE)]
             step5.append(copy(ref, ref, send5.at[i, e], recv5.at[i, e], sibling))
     for c in step5:
         c.wait_recv()
@@ -380,13 +388,13 @@
 
     def half(j, jj, side):
         n = where[j, jj]
-        v = red_ref[pl.ds(64 * (n // 2), 64), :]
+        v = jnp.concatenate([red_ref[pl.ds(768 * i + 32 * (n // 2), 32), :] for i in range(2)], axis=0)
         return v if n % 2 == side else pltpu.roll(v, 64, 1)
 
     for j in range(8):
         for pair in range(j // 2, 5):
             if pair == 4:
-                r = jnp.broadcast_to(red_ref[pl.ds(1408 + j, 1), :], (64, 128))
+                r = jnp.broadcast_to(red_ref[pl.ds(704 + j, 1), :], (64, 128))
                 drive = jnp.sum(jnp.where(lane == sub, r, 0.0), axis=1, keepdims=True)
                 u = jnp.where(lane < 64, half(j, 8, 0), jnp.where(lane == 64, drive, 0.0))
             elif 2 * pair < j:
@@ -414,10 +422,13 @@
             w_s[pl.ds(at, 128), pl.ds(at + 128, 384 - at)], w_s[pl.ds(at + 128, 384 - at), pl.ds(512, 128)])
 
 
-def update_kernel(red_ref, modes_ref, mem_hbm, inc_ref, ana_hbm, a_s, w_s, phi_s, u_s, big_s, mem_s, ana_s, load_sem, save_sem):
+def update_kernel(red_hbm, modes_ref, mem_hbm, inc_ref, ana_hbm, red_s, a_s, w_s, phi_s, u_s, big_s, mem_s, ana_s, red_sem, load_sem, save_sem):
+    red_load = pltpu.make_async_copy(red_hbm, red_s, red_sem)
+    red_load.start()
     load = pltpu.make_async_copy(mem_hbm, mem_s, load_sem)
     load.start()
-    solve(red_ref, a_s, w_s)
+    red_load.wait()
+    solve(red_s, a_s, w_s)
     shift = lax.rem(128 - lax.axis_index("band") * 16, 128)
     phi = pltpu.roll(modes_ref[...], shift, 1)
     lane = lax.broadcasted_iota(jnp.int32, (8, 128), 1)
@@ -455,11 +466,11 @@
 
 def per_device(members, modes, *obs):
     flat = members.reshape(1024, 2048)
-    anywhere = pl.BlockSpec(memory_space=pl.ANY)
+    in_hbm = pl.BlockSpec(memory_space=pl.ANY)
     red = pl.pallas_call(
         front_kernel,
         out_shape=jax.ShapeDtypeStruct((ROWS, 128), F32),
-        in_specs=[anywhere] * 7 + [pl.BlockSpec(memory_space=pltpu.SMEM)],
+        in_specs=[in_hbm] * 7 + [pl.BlockSpec(memory_space=pltpu.SMEM)],
         out_specs=VM,
         scratch_shapes=[pltpu.VMEM((64, 128), jnp.int32)] * 3
         + [pltpu.VMEM((64, 128), F32)] * 3
@@ -476,8 +487,8 @@
             pltpu.VMEM((2, 64, 2048), BF),
             pltpu.VMEM((2, 64, 2048), BF),
             pltpu.VMEM((ROWS, 128), F32),
-            pltpu.VMEM((HALF, 128), F32),
-            pltpu.VMEM((HALF, 128), F32),
+            pltpu.VMEM((2, PART, 128), F32),
+            pltpu.VMEM((2, PART, 128), F32),
             pltpu.VMEM((2, 16, PIECE, 128), F32),
             pltpu.VMEM((2, 8, PIECE, 128), F32),
             pltpu.SemaphoreType.DMA((6,)),
@@ -486,16 +497,17 @@
         + [pltpu.SemaphoreType.DMA(n) for n in ((2,), (2,), (2,), (2,))]
         + [pltpu.SemaphoreType.DMA((2, n)) for n in (16, 16, 8, 8, 16, 16, 16, 16)],
         compiler_params=pltpu.CompilerParams(
-            collective_id=0, has_side_effects=True, vmem_limit_bytes=56 * 2**20
+            collective_id=0, has_side_effects=True, vmem_limit_bytes=60 * 2**20
         ),
         name="front",
     )(*[o.reshape(64, 128) for o in obs], flat, modes)
     inc, ana = pl.pallas_call(
         update_kernel,
         out_shape=(jax.ShapeDtypeStruct((16, 2048), F32), jax.ShapeDtypeStruct((1024, 2048), BF)),
-        in_specs=[VM, VM, anywhere],
-        out_specs=(VM, anywhere),
+        in_specs=[in_hbm, VM, in_hbm],
+        out_specs=(VM, in_hbm),
         scratch_shapes=[
+            pltpu.VMEM((ROWS, 128), F32),
             pltpu.VMEM((512, 640), F32),
             pltpu.VMEM((512, 640), F32),
             pltpu.VMEM((512, 1024), F32),
@@ -504,9 +516,10 @@
             pltpu.VMEM((1024, 2048), BF),
             pltpu.VMEM((1024, 2048), BF),
             pltpu.SemaphoreType.DMA,
+            pltpu.SemaphoreType.DMA,
             pltpu.SemaphoreType.DMA((4,)),
         ],
-        compiler_params=pltpu.CompilerParams(vmem_limit_bytes=48 * 2**20),
+        compiler_params=pltpu.CompilerParams(vmem_limit_bytes=60 * 2**20),
         name="update",
     )(red, modes, flat)
     return inc, ana.reshape(64, 16, 2048)

time: 83.2 us -> 78.4 us (0.942)
  Pallas kernels: 81 us -> 77.5 us
  local copies, waits for them, and re-layouts: 1.13 us -> 0 us
    pallas_call x1, Pallas kernels: 53.1 us -> 48.2 us  [per_device(): pl.pallas_call(front_kernel, out_shape=jax.ShapeDtypeStruct((ROWS, 128),...]
    pallas_call x1, Pallas kernels: 27.9 us -> 29.3 us  [per_device(): pl.pallas_call(update_kernel, out_shape=(jax.ShapeDtypeStruct((16, 2048),...]
    unnamed x6 -> x0, local copies, waits for them, and re-layouts: 1.13 us -> none
where the time goes in v3:
time: 78.4 us; the launch traced here: 78.3 us
  Pallas kernels  77.5 us (99%)
  between operations  0.82 us (1%)
    pallas_call x1, Pallas kernels, per_device(): pl.pallas_call(front_kernel, out_shape=jax.ShapeDtypeStruct((ROWS, 128),...  48.2 us
    pallas_call x1, Pallas kernels, per_device(): pl.pallas_call(update_kernel, out_shape=(jax.ShapeDtypeStruct((16, 2048),...  29.3 us

profile of v3, /device:TPU:1, one launch (start us, length us, event | category | flops | bytes accessed | tf_op | source)
XLA Modules:
  0.0 78.3 jit_solution(6145635580147915930)
XLA Ops:
  0.6 48.2 %front.1.red_hbm = f32[1536,128]{1,0:T(8,128)} custom-call(s32[64,128]{1,0:T(8,128)} %bitcast.10, s32[64,128]{1,0:T(8,128)} %bitcast.11, s32[64,128]{1,0:T(8,128)} %bitcast.12, f32[64,128]{1,0:T(8,128)} %bitcast.13, f32[64,128]{1,0:T(8,128)} %bitcast.14, f32[64,128]{1,0:T(8,128)} %bitcast.15, bf16[1024,2048]{1,0:T(8,128)(2,1)} %bitcast.8, f32[8,128]{1,0:T(8,128)} %modes_ref.3), custom_call_target="tpu_custom_call" | custom-call | tf_op jit(solution)/shard_map/front/pallas_call | solution.py:470
  48.8 29.3 %update.1 = (f32[16,2048]{1,0:T(8,128)}, bf16[1024,2048]{1,0:T(8,128)(2,1)}) custom-call(f32[1536,128]{1,0:T(8,128)} %front.1.red_hbm, f32[8,128]{1,0:T(8,128)} %modes_ref.3, bf16[1024,2048]{1,0:T(8,128)(2,1)} %bitcast.9), custom_call_target="tpu_custom_call" | custom-call | tf_op jit(solution)/shard_map/update/pallas_call | solution.py:504

commit v4 on v3

--- a/solution.py
+++ b/solution.py
@@ -243,11 +243,12 @@
     sibling = dev(x, y, z, 1 - core)
     up = (tile, (band + 1) % 8)
     down = (tile, (band + 7) % 8)
-    partners = [up, down]
-    for e in range(1, 16):
+    partners = [dev(x, y, (z + e) % 8, core) for e in (4, 3, 5)]
+    for e in order:
         partners.append(dev(*plane(e), z, core))
-    for e in range(1, 8):
+    for e in (2, 6, 1, 7):
         partners.append(dev(x, y, (z + e) % 8, core))
+    partners += [up, down]
     barrier = pltpu.get_barrier_semaphore()
     for d in partners:
         pl.semaphore_signal(barrier, inc=1, device_id=d, device_id_type=pl.DeviceIdType.MESH)

time: 78.4 us -> 78.4 us (level)
  no operation moved by 1% of the time
where the time goes in v4:
time: 78.4 us; the launch traced here: 78.3 us
  Pallas kernels  77.4 us (99%)
  between operations  0.82 us (1%)
    pallas_call x1, Pallas kernels, per_device(): pl.pallas_call(front_kernel, out_shape=jax.ShapeDtypeStruct((ROWS, 128),...  48.2 us
    pallas_call x1, Pallas kernels, per_device(): pl.pallas_call(update_kernel, out_shape=(jax.ShapeDtypeStruct((16, 2048),...  29.3 us

profile of v4, /device:TPU:1, one launch (start us, length us, event | category | flops | bytes accessed | tf_op | source)
XLA Modules:
  0.0 78.3 jit_solution(15111678175216952250)
XLA Ops:
  0.6 48.2 %front.1.red_hbm = f32[1536,128]{1,0:T(8,128)} custom-call(s32[64,128]{1,0:T(8,128)} %bitcast.10, s32[64,128]{1,0:T(8,128)} %bitcast.11, s32[64,128]{1,0:T(8,128)} %bitcast.12, f32[64,128]{1,0:T(8,128)} %bitcast.13, f32[64,128]{1,0:T(8,128)} %bitcast.14, f32[64,128]{1,0:T(8,128)} %bitcast.15, bf16[1024,2048]{1,0:T(8,128)(2,1)} %bitcast.8, f32[8,128]{1,0:T(8,128)} %modes_ref.3), custom_call_target="tpu_custom_call" | custom-call | tf_op jit(solution)/shard_map/front/pallas_call | solution.py:471
  48.8 29.3 %update.1 = (f32[16,2048]{1,0:T(8,128)}, bf16[1024,2048]{1,0:T(8,128)(2,1)}) custom-call(f32[1536,128]{1,0:T(8,128)} %front.1.red_hbm, f32[8,128]{1,0:T(8,128)} %modes_ref.3, bf16[1024,2048]{1,0:T(8,128)(2,1)} %bitcast.9), custom_call_target="tpu_custom_call" | custom-call | tf_op jit(solution)/shard_map/update/pallas_call | solution.py:505
